TPU v7x, 256 devices: a whole 4x4x8 slice. The times are simulated.
256 devices in a mesh: grp: 16 (over x, y), dev: 16 (over z, core).
Axes of the slice: x: 4, y: 4, z: 8, core: 2. Of those that a mesh axis runs over, the one named last changes fastest.
Arguments:
- features: bfloat16 [2048, 8, 8, 512], P(('grp', 'dev')), may hold values from -6 to 6
- cotangent: bfloat16 [2048, 8, 8, 512], P(('grp', 'dev')), may hold values from -6 to 6
- timesteps: int32 [2048], P(('grp', 'dev')), may hold values from 0 to 999
- face_links: int32 [2048, 6], P(('grp', 'dev')), may hold values from -1 to 39
- face_sources: int32 [256, 16, 2], P(('grp', 'dev')), may hold values from -1 to 47, as said below
- coarse_targets: int32 [2048], P(('grp', 'dev')), may hold values from 0 to 15, as said below
- coarse_places: int32 [256, 16, 1], P(('grp', 'dev')), may hold values from -1 to 63, as said below
- time_weight: float32 [64, 128], replicated, may hold values from -0.75 to 0.75
- fine_weight: bfloat16 [7, 64, 64], replicated, may hold values from -0.25 to 0.25
- down_weight: bfloat16 [64, 128], replicated, may hold values from -2 to 2
- coarse_weight: bfloat16 [7, 128, 128], replicated, may hold values from -0.1875 to 0.1875
- up_weight: bfloat16 [128, 64], replicated, may hold values from -1 to 1
Outputs:
- mixed_out: bfloat16 [2048, 8, 8, 512], P(('grp', 'dev'))
- input_grad: bfloat16 [2048, 8, 8, 512], P(('grp', 'dev'))
- fine_grad: float32 [7, 64, 64], replicated
- down_grad: float32 [64, 128], replicated
- coarse_grad: float32 [7, 128, 128], replicated
- up_grad: float32 [128, 64], replicated
- time_grad: float32 [64, 128], replicated
Inputs may be any that keep to these rules, and one draw needn't show every extreme that they name: `face_sources`: -1 marks an unused slot; a used slot names brick * 6 + side of the providing device. `coarse_targets`: each brick names one slot, each slot at most one brick; some owners of each group receive all 1 slots from every device of the group. `coarse_places`: -1 exactly for slots that no brick names; used positions are distinct on each owner.
All inputs are finite; a program needn't handle non-finite values.
Results may differ from a plain program's by a relative error of at most 0.014.
Values may be sent and summed in bfloat16 or wider, within the bound.
A program may use at most 128 MiB of HBM per device.

v0:
```python
import math

import jax
import jax.numpy as jnp
from jax import lax
from jax.sharding import PartitionSpec as P

GROUPS = 32
COARSE_DEV = 1


OPPOSITE = (1, 0, 3, 2, 5, 4)
EPSILON = 1e-05


def brick_view(packed):
    return packed.reshape(packed.shape[0], 8, 8, 8, packed.shape[-1] // 8)


def time_embedding(step_ids, channels):
    half_width = channels // 2
    frequency = jnp.exp(
        -math.log(10000.0) * jnp.arange(half_width).astype(jnp.float32) / half_width
    )
    angles = step_ids.astype(jnp.float32)[:, None] * frequency[None, :]
    return jnp.concatenate([jnp.cos(angles), jnp.sin(angles)], axis=1)


def activate(packed, step_ids, time_weight, groups):
    volume = brick_view(packed).astype(jnp.float32)
    brick_count = volume.shape[0]
    channels = volume.shape[-1]
    grouped = volume.reshape(brick_count, 512, groups, channels // groups)
    centre_mean = jnp.mean(grouped, axis=(1, 3), keepdims=True)
    spread = jnp.mean(jnp.square(grouped - centre_mean), axis=(1, 3), keepdims=True)
    inverse = lax.rsqrt(spread + EPSILON)
    normed = ((grouped - centre_mean) * inverse).reshape(brick_count, 8, 8, 8, channels)
    embedding = time_embedding(step_ids, channels)
    modulate = jnp.dot(embedding, time_weight, precision=lax.Precision.HIGHEST)
    scale_term = modulate[:, :channels][:, None, None, None, :]
    shift_term = modulate[:, channels:][:, None, None, None, :]
    before = normed * (1.0 + scale_term) + shift_term
    return (before, normed, inverse, embedding, scale_term)


def face_table(volume):
    layers = [
        volume[:, 0],
        volume[:, 7],
        volume[:, :, 0],
        volume[:, :, 7],
        volume[:, :, :, 0],
        volume[:, :, :, 7],
    ]
    return jnp.stack(layers, axis=1)


def add_faces(volume, layers):
    volume = volume.at[:, 0].add(layers[:, 0])
    volume = volume.at[:, 7].add(layers[:, 1])
    volume = volume.at[:, :, 0].add(layers[:, 2])
    volume = volume.at[:, :, 7].add(layers[:, 3])
    volume = volume.at[:, :, :, 0].add(layers[:, 4])
    volume = volume.at[:, :, :, 7].add(layers[:, 5])
    return volume


def padded_volume(volume, layers):
    brick_count = volume.shape[0]
    channels = volume.shape[-1]
    padded = jnp.zeros((brick_count, 10, 10, 10, channels), volume.dtype)
    padded = padded.at[:, 1:9, 1:9, 1:9].set(volume)
    padded = padded.at[:, 0, 1:9, 1:9].set(layers[:, 0])
    padded = padded.at[:, 9, 1:9, 1:9].set(layers[:, 1])
    padded = padded.at[:, 1:9, 0, 1:9].set(layers[:, 2])
    padded = padded.at[:, 1:9, 9, 1:9].set(layers[:, 3])
    padded = padded.at[:, 1:9, 1:9, 0].set(layers[:, 4])
    padded = padded.at[:, 1:9, 1:9, 9].set(layers[:, 5])
    return padded


def tap_stack(padded, direction_sign):
    pieces = [padded[:, 1:9, 1:9, 1:9]]
    for direction in range(6):
        offset = 1 + direction_sign * (2 * (direction % 2) - 1)
        starts = [1, 1, 1]
        starts[direction // 2] = offset
        pieces.append(
            padded[
                :, starts[0] : starts[0] + 8, starts[1] : starts[1] + 8, starts[2] : starts[2] + 8
            ]
        )
    return jnp.concatenate(pieces, axis=-1)


def pick_rows(values, indices):
    zero_row = jnp.zeros((1,) + values.shape[1:], values.dtype)
    return jnp.concatenate([values, zero_row], axis=0)[indices]


def slot_bricks(targets, slot_count):
    brick_count = targets.shape[0]
    return jnp.full((slot_count,), brick_count, jnp.int32).at[targets].set(jnp.arange(brick_count))


def place_slots(places, place_count):
    slot_count = places.size
    flat_places = places.reshape(-1)
    target = jnp.where(flat_places < 0, place_count, flat_places)
    filled = (
        jnp.full((place_count + 1,), slot_count, jnp.int32).at[target].set(jnp.arange(slot_count))
    )
    return filled[:place_count]


def places_to_grid(placed, coarse_count):
    channels = placed.shape[-1]
    shaped = placed.reshape(coarse_count, 4, 4, 4, 2, 2, 2, channels)
    return shaped.transpose(0, 1, 4, 2, 5, 3, 6, 7).reshape(coarse_count, 8, 8, 8, channels)


def grid_to_places(volume):
    coarse_count = volume.shape[0]
    channels = volume.shape[-1]
    shaped = volume.reshape(coarse_count, 4, 2, 4, 2, 4, 2, channels)
    return shaped.transpose(0, 1, 3, 5, 2, 4, 6, 7).reshape(coarse_count * 64, 8, channels)


def pool_bricks(volume):
    brick_count = volume.shape[0]
    channels = volume.shape[-1]
    shaped = volume.reshape(brick_count, 2, 4, 2, 4, 2, 4, channels)
    return jnp.mean(shaped, axis=(2, 4, 6)).reshape(brick_count, 8, channels)


def spread_bricks(values):
    brick_count = values.shape[0]
    channels = values.shape[-1]
    shaped = values.reshape(brick_count, 2, 1, 2, 1, 2, 1, channels)
    return jnp.broadcast_to(shaped, (brick_count, 2, 4, 2, 4, 2, 4, channels)).reshape(
        brick_count, 8, 8, 8, channels
    )


def gather_halo(face_rows, received, links):
    brick_count = links.shape[0]
    zero_row = jnp.zeros((1,) + face_rows.shape[1:], face_rows.dtype)
    every_face = jnp.concatenate([face_rows, received, zero_row], axis=0)
    opposite = jnp.array(OPPOSITE, jnp.int32)[None, :]
    local_index = links * 6 + opposite
    remote_index = brick_count * 6 + links - brick_count
    empty_index = every_face.shape[0] - 1
    indices = jnp.where(
        links < 0, empty_index, jnp.where(links < brick_count, local_index, remote_index)
    )
    return every_face[indices]


def coarse_forward(incoming, places, down_weight, coarse_weight, coarse_count):
    channels = down_weight.shape[0]
    coarse_width = down_weight.shape[1]
    slot_of_place = place_slots(places, coarse_count * 64)
    pooled_places = pick_rows(incoming, slot_of_place).reshape(coarse_count * 64, 8, channels)
    flat_pooled = places_to_grid(pooled_places, coarse_count).reshape(-1, channels)
    coarse_pre = jnp.dot(flat_pooled, down_weight, preferred_element_type=jnp.float32)
    coarse_act = jax.nn.silu(coarse_pre).astype(jnp.bfloat16)
    act_grid = coarse_act.reshape(coarse_count, 8, 8, 8, coarse_width)
    empty_faces = jnp.zeros((coarse_count, 6, 8, 8, coarse_width), jnp.bfloat16)
    coarse_stack = tap_stack(padded_volume(act_grid, empty_faces), 1).reshape(-1, 7 * coarse_width)
    coarse_out = jnp.dot(
        coarse_stack,
        coarse_weight.reshape(7 * coarse_width, coarse_width),
        preferred_element_type=jnp.float32,
    ).astype(jnp.bfloat16)
    return (flat_pooled, coarse_pre, coarse_stack, coarse_out)


def coarse_send(coarse_out, places, coarse_count):
    coarse_width = coarse_out.shape[-1]
    coarse_rows = grid_to_places(coarse_out.reshape(coarse_count, 8, 8, 8, coarse_width)).reshape(
        coarse_count * 64, 8 * coarse_width
    )
    return pick_rows(coarse_rows, jnp.where(places < 0, coarse_count * 64, places))


def coarse_backward(
    incoming_grad,
    places,
    flat_pooled,
    coarse_pre,
    coarse_stack,
    up_weight,
    down_weight,
    coarse_weight,
    coarse_count,
):
    channels = down_weight.shape[0]
    coarse_width = down_weight.shape[1]
    slot_of_place = place_slots(places, coarse_count * 64)
    grad_places = pick_rows(incoming_grad, slot_of_place).reshape(coarse_count * 64, 8, channels)
    grad_grid = places_to_grid(grad_places, coarse_count).reshape(-1, channels)
    grad_out = jnp.dot(grad_grid, up_weight.astype(jnp.float32).T, precision=lax.Precision.HIGHEST)
    coarse_grad = lax.dot_general(
        coarse_stack.astype(jnp.float32),
        grad_out,
        (((0,), (0,)), ((), ())),
        precision=lax.Precision.HIGHEST,
    ).reshape(7, coarse_width, coarse_width)
    empty_faces = jnp.zeros((coarse_count, 6, 8, 8, coarse_width), jnp.float32)
    grad_stack = tap_stack(
        padded_volume(grad_out.reshape(coarse_count, 8, 8, 8, coarse_width), empty_faces), -1
    ).reshape(-1, 7 * coarse_width)
    flipped = (
        coarse_weight.astype(jnp.float32).transpose(0, 2, 1).reshape(7 * coarse_width, coarse_width)
    )
    grad_act = jnp.dot(grad_stack, flipped, precision=lax.Precision.HIGHEST)
    sigmoid_term = jax.nn.sigmoid(coarse_pre)
    grad_pre = grad_act * sigmoid_term * (1.0 + coarse_pre * (1.0 - sigmoid_term))
    down_grad = jnp.dot(
        flat_pooled.astype(jnp.float32).T, grad_pre, precision=lax.Precision.HIGHEST
    )
    grad_pooled = jnp.dot(
        grad_pre, down_weight.astype(jnp.float32).T, precision=lax.Precision.HIGHEST
    )
    back_rows = grid_to_places(grad_pooled.reshape(coarse_count, 8, 8, 8, channels)).reshape(
        coarse_count * 64, 8 * channels
    )
    return (
        pick_rows(back_rows, jnp.where(places < 0, coarse_count * 64, places)),
        coarse_grad,
        down_grad,
    )


def rim_gradients(grad_view, fine_weight):
    brick_count = grad_view.shape[0]
    channels = grad_view.shape[-1]
    grad_faces = face_table(grad_view)
    rim_list = []
    for direction in range(6):
        grad_layer = grad_faces[:, direction].reshape(brick_count * 64, channels)
        product = jnp.dot(
            grad_layer, fine_weight[direction + 1].T, preferred_element_type=jnp.float32
        )
        rim_list.append(product.reshape(brick_count, 8, 8 * channels))
    return jnp.stack(rim_list, axis=1).reshape(brick_count * 6, 8, 8 * channels)


def local_face_grads(rim_rows, links):
    brick_count = links.shape[0]
    opposite = jnp.array(OPPOSITE, jnp.int32)[None, :]
    is_local = (links >= 0) & (links < brick_count)
    target = jnp.where(is_local, links * 6 + opposite, brick_count * 6).reshape(-1)
    empty_table = jnp.zeros((brick_count * 6 + 1,) + rim_rows.shape[1:], jnp.float32)
    return empty_table.at[target].add(rim_rows)


def slot_pairs(links, slot_count):
    brick_count = links.shape[0]
    remote = jnp.where(links >= brick_count, links - brick_count, slot_count).reshape(-1)
    filled = (
        jnp.full((slot_count + 1,), brick_count * 6, jnp.int32)
        .at[remote]
        .set(jnp.arange(brick_count * 6))
    )
    return filled[:slot_count]


def transposed_conv(grad_view, fine_weight):
    brick_count = grad_view.shape[0]
    channels = grad_view.shape[-1]
    empty_faces = jnp.zeros((brick_count, 6, 8, 8, channels), grad_view.dtype)
    grad_stack = tap_stack(padded_volume(grad_view, empty_faces), -1).reshape(
        brick_count * 512, 7 * channels
    )
    flipped = fine_weight.transpose(0, 2, 1).reshape(7 * channels, channels)
    return jnp.dot(grad_stack, flipped, preferred_element_type=jnp.float32).reshape(
        brick_count, 8, 8, 8, channels
    )


def finish_backward(grad_active, before, normed, inverse, embedding, scale_term, grad_view, groups):
    brick_count = before.shape[0]
    channels = before.shape[-1]
    sigmoid_term = jax.nn.sigmoid(before)
    grad_before = grad_active * sigmoid_term * (1.0 + before * (1.0 - sigmoid_term))
    grad_scale = jnp.sum(grad_before * normed, axis=(1, 2, 3))
    grad_shift = jnp.sum(grad_before, axis=(1, 2, 3))
    time_grad = jnp.dot(
        embedding.T,
        jnp.concatenate([grad_scale, grad_shift], axis=1),
        precision=lax.Precision.HIGHEST,
    )
    grad_normed = (grad_before * (1.0 + scale_term)).reshape(
        brick_count, 512, groups, channels // groups
    )
    grouped_norm = normed.reshape(brick_count, 512, groups, channels // groups)
    centred = grad_normed - jnp.mean(grad_normed, axis=(1, 3), keepdims=True)
    grad_input = inverse * (
        centred - grouped_norm * jnp.mean(grad_normed * grouped_norm, axis=(1, 3), keepdims=True)
    )
    grad_total = grad_view.astype(jnp.float32) + grad_input.reshape(brick_count, 8, 8, 8, channels)
    return (grad_total.astype(jnp.bfloat16).reshape(brick_count, 8, 8, 8 * channels), time_grad)


def body(
    features,
    cotangent,
    timesteps,
    face_links,
    face_sources,
    coarse_targets,
    coarse_places,
    time_weight,
    fine_weight,
    down_weight,
    coarse_weight,
    up_weight,
):
    brick_count = features.shape[0]
    channels = features.shape[-1] // 8
    coarse_width = down_weight.shape[1]
    sources = face_sources[0]
    places = coarse_places[0]
    peer_count = sources.shape[0]
    face_total = sources.size
    slot_total = places.size
    before, normed, inverse, embedding, scale_term = activate(
        features, timesteps, time_weight, GROUPS
    )
    active = jax.nn.silu(before).astype(jnp.bfloat16)
    face_rows = face_table(active).reshape(brick_count * 6, 8, 8 * channels)
    outgoing = pick_rows(face_rows, jnp.where(sources < 0, brick_count * 6, sources))
    arrived = lax.all_to_all(outgoing, "dev", split_axis=0, concat_axis=0, tiled=True)
    halo_layers = gather_halo(face_rows, arrived.reshape(-1, 8, 8 * channels), face_links).reshape(
        brick_count, 6, 8, 8, channels
    )
    pooled = pool_bricks(active.astype(jnp.float32)).astype(jnp.bfloat16)
    slot_owner = slot_bricks(coarse_targets, slot_total)
    pooled_out = pick_rows(pooled.reshape(brick_count, 8 * channels), slot_owner).reshape(
        peer_count, -1, 8 * channels
    )
    pooled_in = lax.all_to_all(pooled_out, "dev", split_axis=0, concat_axis=0, tiled=True)
    flat_pooled, coarse_pre, coarse_stack, coarse_out = coarse_forward(
        pooled_in.reshape(slot_total, 8 * channels), places, down_weight, coarse_weight, COARSE_DEV
    )
    back_out = coarse_send(coarse_out, places, COARSE_DEV)
    back_in = lax.all_to_all(back_out, "dev", split_axis=0, concat_axis=0, tiled=True)
    coarse_values = back_in.reshape(slot_total, 8, coarse_width)[coarse_targets]
    grad_view = brick_view(cotangent)
    grad_flat = grad_view.reshape(-1, channels)
    full_stack = tap_stack(padded_volume(active, halo_layers), 1).reshape(
        brick_count * 512, 7 * channels
    )
    conv_out = jnp.dot(
        full_stack, fine_weight.reshape(7 * channels, channels), preferred_element_type=jnp.float32
    ).reshape(brick_count, 8, 8, 8, channels)
    fine_grad = lax.dot_general(
        full_stack, grad_flat, (((0,), (0,)), ((), ())), preferred_element_type=jnp.float32
    ).reshape(7, channels, channels)
    upward = jnp.dot(
        coarse_values.reshape(brick_count * 8, coarse_width),
        up_weight,
        preferred_element_type=jnp.float32,
    ).reshape(brick_count, 8, channels)
    result = brick_view(features).astype(jnp.float32) + conv_out + spread_bricks(upward)
    mixed_out = result.astype(jnp.bfloat16).reshape(features.shape)
    grad_up = jnp.sum(
        grad_view.astype(jnp.float32).reshape(brick_count, 2, 4, 2, 4, 2, 4, channels),
        axis=(2, 4, 6),
    ).reshape(brick_count, 8, channels)
    up_grad = jnp.dot(
        coarse_values.reshape(-1, coarse_width).astype(jnp.float32).T,
        grad_up.reshape(-1, channels),
        precision=lax.Precision.HIGHEST,
    )
    grad_send = pick_rows(grad_up.reshape(brick_count, 8 * channels), slot_owner).reshape(
        peer_count, -1, 8 * channels
    )
    grad_arrive = lax.all_to_all(
        grad_send.astype(jnp.bfloat16), "dev", split_axis=0, concat_axis=0, tiled=True
    ).astype(grad_send.dtype)
    grad_back, coarse_grad, down_grad = coarse_backward(
        grad_arrive.reshape(slot_total, 8 * channels),
        places,
        flat_pooled,
        coarse_pre,
        coarse_stack,
        up_weight,
        down_weight,
        coarse_weight,
        COARSE_DEV,
    )
    pooled_back = lax.all_to_all(
        grad_back.astype(jnp.bfloat16), "dev", split_axis=0, concat_axis=0, tiled=True
    ).astype(grad_back.dtype)
    pooled_grad = pooled_back.reshape(slot_total, 8, channels)[coarse_targets]
    grad_active = transposed_conv(grad_view, fine_weight)
    rim_rows = rim_gradients(grad_view, fine_weight)
    face_grad = local_face_grads(rim_rows, face_links)
    pair_of_slot = slot_pairs(face_links, face_total)
    flat_sources = sources.reshape(-1)
    returned = pick_rows(rim_rows, pair_of_slot).reshape(peer_count, -1, 8, 8 * channels)
    came_back = lax.all_to_all(
        returned.astype(jnp.bfloat16), "dev", split_axis=0, concat_axis=0, tiled=True
    ).astype(returned.dtype)
    arriving = came_back.reshape(face_total, 8, 8 * channels)
    source_target = jnp.where(flat_sources < 0, brick_count * 6, flat_sources)
    face_grad = face_grad.at[source_target].add(arriving)
    grad_active = add_faces(
        grad_active, face_grad[: brick_count * 6].reshape(brick_count, 6, 8, 8, channels)
    )
    grad_active = grad_active + spread_bricks(pooled_grad) / 64.0
    input_grad, time_grad = finish_backward(
        grad_active, before, normed, inverse, embedding, scale_term, grad_view, GROUPS
    )
    weight_sums = lax.psum((fine_grad, down_grad, coarse_grad, up_grad, time_grad), ("grp", "dev"))
    return (
        mixed_out,
        input_grad,
        weight_sums[0],
        weight_sums[1],
        weight_sums[2],
        weight_sums[3],
        weight_sums[4],
    )


def solution(mesh):
    in_specs = (
        P(("grp", "dev"), None, None, None),
        P(("grp", "dev"), None, None, None),
        P(("grp", "dev")),
        P(("grp", "dev"), None),
        P(("grp", "dev"), None, None),
        P(("grp", "dev")),
        P(("grp", "dev"), None, None),
        P(),
        P(),
        P(),
        P(),
        P(),
    )
    out_specs = (
        P(("grp", "dev"), None, None, None),
        P(("grp", "dev"), None, None, None),
        P(),
        P(),
        P(),
        P(),
        P(),
    )
    return jax.shard_map(body, mesh=mesh, in_specs=in_specs, out_specs=out_specs, check_vma=False)
```

profile of v0, /device:TPU:1, one launch (start us, length us, event | category | flops | bytes accessed | tf_op | source)
XLA Modules:
  0.0 806.8 jit_solution(10224148169818433437)
XLA Ops:
  7.2 9.7 %copy.178 = f32[8,8,8,512]{0,3,2,1:T(8,128)} copy(bf16[8,8,8,512]{3,2,1,0:T(8,128)(2,1)} %param.82) | data formatting | bytes 1572864 | tf_op jit(solution)/shard_map/convert_element_type | solution.py:366
  18.8 10.5 %reduce_sum.86 = f32[8,32]{0,1:T(8,128)S(1)} reduce(f32[8,512,32,2]{0,3,2,1:T(2,128)} %bitcast.225, f32[]{:T(128)} %constant.888.clone.1), dimensions={1,3}, to_apply=%region_0.0 | reduce | flops 261888 | bytes 1049604 | tf_op jit(solution)/shard_map/reduce_sum | solution.py:34
  29.3 13.5 %multiply_reduce_fusion = f32[8,32]{0,1:T(8,128)S(1)} fusion(f32[8,512,32,2]{0,3,2,1:T(2,128)} %bitcast.226, f32[8,32]{0,1:T(8,128)S(1)} %broadcast_multiply_fusion.3), kind=kLoop, calls=%fused_computation.16 | loop fusion | flops 786176 | bytes 1050624 | tf_op jit(solution)/shard_map/reduce_sum | solution.py:35
  48.8 10.0 %all-to-all-start.1 = ((bf16[16,2,256]{2,1,0:T(2,128)(2,1)}), bf16[16,2,256]{2,1,0:T(2,128)(2,1)}, u32[]{:S(2)}, u32[]{:S(2)}) async-start(bf16[16,2,256]{2,1,0:T(2,128)(2,1)} %reshape.1948), calls=%async_computation.1 | async-start | bytes 32768 | tf_op jit(solution)/shard_map/all_to_all | solution.py:343
  62.2 2.1 scatter.140
  92.5 6.4 scatter.149
  98.9 6.4 scatter.150
  105.3 3.4 fusion.60
  116.0 9.7 %concatenate.135 = bf16[8,8,8,8,448]{4,3,2,1,0:T(8,128)(2,1)} concatenate(bf16[8,8,8,8,64]{4,3,2,1,0:T(8,128)(2,1)} %get-tuple-element.431, bf16[8,8,8,8,64]{4,3,2,1,0:T(8,128)(2,1)} %get-tuple-element.430, bf16[8,8,8,8,64]{4,3,2,1,0:T(8,128)(2,1)} %get-tuple-element.429, bf16[8,8,8,8,64]{4,3,2,1,0:T(8,128)(2,1)} %get-tuple-element.428, ...), dimensions={4} | concatenate | bytes 7340032 | tf_op jit(solution)/shard_map/concatenate | solution.py:93
  125.7 4.8 fusion.16
  131.6 2.4 reshape.1788
  137.7 2.2 reduce_sum.89
  143.6 4.8 scatter_fusion
  150.4 7.2 all-to-all-start.4
  162.9 2.0 convolution_convert_fusion
  164.9 2.2 copy.224
  183.0 2.0 fusion.1
  190.4 7.2 all-to-all-start.5
  197.6 2.9 fusion.10
  204.9 6.7 all-to-all-start.2
  212.5 6.5 all-to-all-done.2
  219.0 4.3 all-to-all-start.3
  225.2 10.0 %all-to-all-done.3 = bf16[16,2,8,512]{3,2,1,0:T(8,128)(2,1)} async-done(((bf16[16,2,8,512]{3,2,1,0:T(8,128)(2,1)}), bf16[16,2,8,512]{3,2,1,0:T(8,128)(2,1)}, u32[]{:S(2)}, u32[]{:S(2)}) %all-to-all-start.3) | async-done | bytes 262176 | tf_op jit(solution)/shard_map/all_to_all | solution.py:404
  239.1 2.5 reshape.1769
  243.4 2.0 fusion.62
  251.0 7.9 scatter-add.50
  258.8 1.9 slice_add_fusion
  260.8 7.9 scatter-add.51
  270.2 3.5 multiply_reduce_fusion.1
  276.2 2.4 reshape.1745
  280.4 2.3 gather_fusion
  282.6 4.1 all-to-all-start
  287.2 4.3 add_convert_fusion
  291.5 2.6 reshape.1780
  295.3 2.3 all-to-all-done
  297.6 2.1 maximum_maximum_fusion
  299.7 2.4 gather_fusion.1
  302.1 2.3 reshape.1747
  304.4 2.0 slice_bitcast_fusion.2
  312.2 6.4 scatter.121
  318.6 6.4 scatter.124
  325.0 3.7 fusion.61
  328.7 10.0 %concatenate.130 = bf16[8,8,8,8,448]{4,3,2,1,0:T(8,128)(2,1)} concatenate(bf16[8,8,8,8,64]{4,3,2,1,0:T(8,128)(2,1)} %get-tuple-element.438, bf16[8,8,8,8,64]{4,3,2,1,0:T(8,128)(2,1)} %get-tuple-element.437, bf16[8,8,8,8,64]{4,3,2,1,0:T(8,128)(2,1)} %get-tuple-element.436, bf16[8,8,8,8,64]{4,3,2,1,0:T(8,128)(2,1)} %get-tuple-element.435, ...), dimensions={4} | concatenate | bytes 7340032 | tf_op jit(solution)/shard_map/concatenate | solution.py:93
  338.7 6.5 copy.222
  345.2 3.9 fusion.2
  350.7 3.5 add_convert_fusion.1
  355.6 181.6 %all-reduce.17.cloned.1.call-done = (f32[64,128]{1,0:T(8,128)}, f32[128,64]{0,1:T(8,128)}, f32[64,128]{1,0:T(8,128)}) async-done(((f32[64,128]{1,0:T(8,128)}, f32[128,64]{0,1:T(8,128)}, f32[64,128]{1,0:T(8,128)}), (f32[64,128]{1,0:T(8,128)}, f32[128,64]{0,1:T(8,128)}, f32[64,128]{1,0:T(8,128)})) %all-reduce.17.cloned.1.call-update) | async-done | bytes 98320 | tf_op jit(solution)/shard_map/psum | solution.py:417
  537.2 254.7 %all-reduce.19.cloned.1.call-done = (f32[7,64,64]{2,1,0:T(8,128)}, f32[7,128,128]{2,1,0:T(8,128)}) async-done(((f32[7,64,64]{2,1,0:T(8,128)}, f32[7,128,128]{2,1,0:T(8,128)}), (f32[7,64,64]{2,1,0:T(8,128)}, f32[7,128,128]{2,1,0:T(8,128)})) %all-reduce.19.cloned.1.call-update) | async-done | bytes 573456 | tf_op jit(solution)/shard_map/psum | solution.py:417
  (313 shorter events, 124.8 us)
Async XLA Ops:
  7.2 11.0 %copy-start = (f32[64,128]{1,0:T(8,128)S(1)}, f32[64,128]{1,0:T(8,128)}, u32[]{:S(2)}) copy-start(f32[64,128]{1,0:T(8,128)} %param.89) | copy-start | bytes 98308
  7.2 9.7 %copy-start.8 = (bf16[8,8,8,512]{3,2,1,0:T(8,128)(2,1)S(1)}, bf16[8,8,8,512]{3,2,1,0:T(8,128)(2,1)}, u32[]{:S(2)}) copy-start(bf16[8,8,8,512]{3,2,1,0:T(8,128)(2,1)} %param.82) | copy-start | bytes 1572868
  16.9 1.1 copy-start.45
  18.8 24.3 %copy-start.28 = (f32[8,64]{1,0:T(8,128)}, f32[8,64]{1,0:T(8,128)S(1)}, u32[]{:S(2)}) copy-start(f32[8,64]{1,0:T(8,128)S(1)} %get-tuple-element.460) | copy-start | bytes 6148
  18.8 24.3 %copy-start.31 = (f32[8,64]{1,0:T(8,128)}, f32[8,64]{1,0:T(8,128)S(1)}, u32[]{:S(2)}) copy-start(f32[8,64]{1,0:T(8,128)S(1)} %get-tuple-element.461) | copy-start | bytes 6148
  42.9 2.1 copy-start.46
  42.9 2.8 copy-start.39
  42.9 15.9 %copy-start.47 = (s32[1,16,1]{1,2,0:T(1,128)S(1)}, s32[1,16,1]{1,2,0:T(1,128)}, u32[]{:S(2)}) copy-start(s32[1,16,1]{1,2,0:T(1,128)} %param.88) | copy-start | bytes 196
  42.9 15.9 %copy-start.10 = (bf16[8,8,8,512]{3,2,1,0:T(8,128)(2,1)S(1)}, bf16[8,8,8,512]{3,2,1,0:T(8,128)(2,1)}, u32[]{:S(2)}) copy-start(bf16[8,8,8,512]{3,2,1,0:T(8,128)(2,1)} %param.83) | copy-start | bytes 1572868
  43.0 16.4 %copy-start.24 = (f32[8,64]{1,0:T(8,128)}, f32[8,64]{1,0:T(8,128)S(1)}, u32[]{:S(2)}) copy-start(f32[8,64]{1,0:T(8,128)S(1)} %copy.180) | copy-start | bytes 6148
  43.1 17.0 %copy-start.26 = (f32[8,64]{1,0:T(8,128)}, f32[8,64]{1,0:T(8,128)S(1)}, u32[]{:S(2)}) copy-start(f32[8,64]{1,0:T(8,128)S(1)} %copy.179) | copy-start | bytes 6148
  46.4 15.7 %copy-start.38 = (s32[1024]{0:T(1024)}, s32[1024]{0:T(1024)S(1)}, u32[]{:S(2)}) copy-start(s32[1024]{0:T(1024)S(1)} %get-tuple-element.470) | copy-start | bytes 12292
  48.8 101.6 %all-to-all-start.1 = ((bf16[16,2,256]{2,1,0:T(2,128)(2,1)}), bf16[16,2,256]{2,1,0:T(2,128)(2,1)}, u32[]{:S(2)}, u32[]{:S(2)}) async-start(bf16[16,2,256]{2,1,0:T(2,128)(2,1)} %reshape.1948), calls=%async_computation.1 | async-start | bytes 32768 | tf_op jit(solution)/shard_map/all_to_all | solution.py:343
  59.4 2.8 copy-start.4
  62.2 2.8 copy-start.40
  62.2 6.9 copy-start.15
  105.3 3.8 copy-start.19
  108.7 7.3 copy-start.13
  125.7 4.8 copy-start.9
  131.6 137.5 %copy-start.2 = (f32[8,8,8,8,64]{4,3,2,1,0:T(8,128)}, f32[8,8,8,8,64]{4,3,2,1,0:T(8,128)S(1)}, u32[]{:S(2)}) copy-start(f32[8,8,8,8,64]{4,3,2,1,0:T(8,128)S(1)} %reshape.1783) | copy-start | bytes 3145732
  136.8 5.8 copy-start.17
  137.7 5.8 copy-start.43
  143.5 15.8 %copy-start.37 = (bf16[64,128]{1,0:T(8,128)(2,1)S(1)}, bf16[64,128]{1,0:T(8,128)(2,1)}, u32[]{:S(2)}) copy-start(bf16[64,128]{1,0:T(8,128)(2,1)} %param.91) | copy-start | bytes 49156
  150.4 16.8 %all-to-all-start.4 = ((bf16[16,2,256]{2,1,0:T(2,128)(2,1)}), bf16[16,2,256]{2,1,0:T(2,128)(2,1)S(1)}, u32[]{:S(2)}, u32[]{:S(2)}) async-start(bf16[16,2,256]{2,1,0:T(2,128)(2,1)} %reshape.1952), calls=%async_computation.4 | async-start | bytes 32768 | tf_op jit(solution)/shard_map/all_to_all | solution.py:380
  162.9 5.3 copy-start.23
  178.5 4.4 copy-start.6
  190.4 14.6 %all-to-all-start.5 = ((bf16[16,2,256]{2,1,0:T(2,128)(2,1)}), bf16[16,2,256]{2,1,0:T(2,128)(2,1)S(1)}, u32[]{:S(2)}, u32[]{:S(2)}) async-start(bf16[16,2,256]{2,1,0:T(2,128)(2,1)} %reshape.1954), calls=%async_computation.5 | async-start | bytes 32768 | tf_op jit(solution)/shard_map/all_to_all | solution.py:394
  197.6 4.7 copy-start.18
  197.6 26.8 %copy-start.22 = (f32[8,2,2,2,64]{4,3,2,1,0:T(2,128)S(1)}, f32[8,2,2,2,64]{4,3,2,1,0:T(2,128)}, u32[]{:S(2)}) copy-start(f32[8,2,2,2,64]{4,3,2,1,0:T(2,128)} %copy-done.21) | copy-start | bytes 49156
  200.5 35.8 %copy-start.42 = (s32[32]{0:T(128)S(1)}, s32[32]{0:T(128)}, u32[]{:S(2)}) copy-start(s32[32]{0:T(128)} %fusion.50) | copy-start | bytes 388
  204.9 14.1 %all-to-all-start.2 = ((bf16[16,2,512]{2,1,0:T(2,128)(2,1)}), bf16[16,2,512]{2,1,0:T(2,128)(2,1)S(1)}, u32[]{:S(2)}, u32[]{:S(2)}) async-start(bf16[16,2,512]{2,1,0:T(2,128)(2,1)} %reshape.1950), calls=%async_computation.2 | async-start | bytes 65536 | tf_op jit(solution)/shard_map/all_to_all | solution.py:348
  219.0 16.3 %all-to-all-start.3 = ((bf16[16,2,8,512]{3,2,1,0:T(8,128)(2,1)}), bf16[16,2,8,512]{3,2,1,0:T(8,128)(2,1)}, u32[]{:S(2)}, u32[]{:S(2)}) async-start(bf16[16,2,8,512]{3,2,1,0:T(8,128)(2,1)} %bitcast.240), calls=%async_computation.3 | async-start | bytes 524288 | tf_op jit(solution)/shard_map/all_to_all | solution.py:404
  250.9 18.1 %copy-start.25 = (f32[8,64]{1,0:T(8,128)S(1)}, f32[8,64]{1,0:T(8,128)}, u32[]{:S(2)}) copy-start(f32[8,64]{1,0:T(8,128)} %copy-done.24) | copy-start | bytes 6148
  250.9 18.1 %copy-start.27 = (f32[8,64]{1,0:T(8,128)S(1)}, f32[8,64]{1,0:T(8,128)}, u32[]{:S(2)}) copy-start(f32[8,64]{1,0:T(8,128)} %copy-done.26) | copy-start | bytes 6148
  250.9 18.1 %copy-start.29 = (f32[8,64]{1,0:T(8,128)S(1)}, f32[8,64]{1,0:T(8,128)}, u32[]{:S(2)}) copy-start(f32[8,64]{1,0:T(8,128)} %copy-done.28) | copy-start | bytes 6148
  250.9 18.1 %copy-start.32 = (f32[8,64]{1,0:T(8,128)S(1)}, f32[8,64]{1,0:T(8,128)}, u32[]{:S(2)}) copy-start(f32[8,64]{1,0:T(8,128)} %copy-done.31) | copy-start | bytes 6148
  268.7 1.6 copy-start.5
  275.2 5.2 copy-start.30
  282.6 15.0 %all-to-all-start = ((bf16[16,2,8,512]{3,2,1,0:T(8,128)(2,1)}), bf16[16,2,8,512]{3,2,1,0:T(8,128)(2,1)}, u32[]{:S(2)}, u32[]{:S(2)}) async-start(bf16[16,2,8,512]{3,2,1,0:T(8,128)(2,1)} %bitcast.241), calls=%async_computation | async-start | bytes 524288 | tf_op jit(solution)/shard_map/all_to_all | solution.py:334
  286.7 250.5 %all-reduce.17.cloned.1.call-start = ((), (), s32[]{:S(2)}) async-start(), calls=%async_computation.6 | async-start | bytes 196608 | tf_op jit(solution)/shard_map/psum | solution.py:417
  287.2 6.8 copy-start.34
  287.2 6.8 copy-start.36
  287.2 10.4 %copy-start.41 = (bf16[81]{0:T(256)(128)(2,1)S(1)}, bf16[81]{0:T(256)(128)(2,1)}, u32[]{:S(2)}) copy-start(bf16[81]{0:T(256)(128)(2,1)} %pad.141.clone) | copy-start | bytes 490
  295.0 496.9 %all-reduce.19.cloned.1.call-start = ((), (), s32[]{:S(2)}) async-start(), calls=%async_computation.7 | async-start | bytes 1376256 | tf_op jit(solution)/shard_map/psum | solution.py:417
  338.7 6.5 copy-start.14
  349.1 1.6 copy-start.3
  349.1 1.6 copy-start.16
  350.7 448.8 %copy-start.1 = (f32[64,128]{1,0:T(8,128)S(1)}, f32[64,128]{1,0:T(8,128)}, u32[]{:S(2)}) copy-start(f32[64,128]{1,0:T(8,128)} %param.89) | copy-start | bytes 98308
  (8 other events, 6.2 us)
Sparse Core Ops, SparseCore 0:
  295.1 242.0 all-reduce.16
  543.4 248.4 all-reduce.18
where the time goes:
time: 819 us; the launch traced here: 807 us
  waiting for transfers between devices  456 us (56%)
  local copies, waits for them, and re-layouts  200 us (24%)
  other arithmetic  63.5 us (8%)
  starting transfers between devices  39.8 us (5%)
  matrix products  32.2 us (4%)
  between operations  15.7 us (2%)
    psum x2, waiting for transfers between devices, body(): lax.psum((fine_grad, down_grad, coarse_grad, up_grad, time_grad), ('grp',...  436 us
    unnamed x138, local copies, waits for them, and re-layouts  30.6 us
    concatenate x4, local copies, waits for them, and re-layouts, tap_stack(): return jnp.concatenate(pieces, axis=-1)  19.8 us
  transfers between devices with their start and end apart: 8, of which 6 were waited for; matrix products, arithmetic and copies ran while one was open for 21% of the time, Pallas kernels for 0%

commit v1 on v0

v1 whole, which is shorter than its diff:
```python
import functools
import math

import jax
import jax.numpy as jnp
import numpy as np
from jax import lax
from jax.experimental import pallas as pl
from jax.experimental.pallas import tpu as pltpu
from jax.sharding import PartitionSpec as P

EPSILON = 1e-05
F32 = jnp.float32
BF16 = jnp.bfloat16
BRICKS = 8
ROWS = 512
LANES = 512
SLOT_ROWS = 16
PART_ROWS = 1280
UNITS = 10


def iota(shape, axis):
    return lax.broadcasted_iota(jnp.int32, shape, axis)


def dot(a, b):
    return jnp.dot(a, b, preferred_element_type=F32)


def dot_nt(a, b):
    return lax.dot_general(a, b, (((1,), (1,)), ((), ())), preferred_element_type=F32)


def dot_tn(a, b):
    return lax.dot_general(a, b, (((0,), (0,)), ((), ())), preferred_element_type=F32)


def one_hot(condition):
    return jnp.where(condition, 1.0, 0.0).astype(BF16)


def lanes_four(v):
    return jnp.concatenate([v, v, v, v], axis=1)


def fold_lanes(v):
    s = (v[:, 0:128] + v[:, 128:256]) + (v[:, 256:384] + v[:, 384:512])
    return s + pltpu.roll(s, 64, 1)


def group_mean(sums):
    s = fold_lanes(sums)
    lane = iota(s.shape, 1)
    pair = jnp.where((lane & 1) == 0, pltpu.roll(s, 127, 1), pltpu.roll(s, 1, 1))
    return lanes_four((s + pair) * (1.0 / 1024.0))


def brick_sum(v):
    return jnp.sum(v.reshape(BRICKS, 64, LANES), axis=1)


def per_brick(v):
    return v[:, None, :]


def face_index(brick, side, r):
    base = brick * 64
    xy = jnp.where(
        side < 0.5,
        base + r,
        jnp.where(
            side < 1.5,
            base + 56 + r,
            jnp.where(side < 2.5, base + 8 * r, base + 8 * r + 7),
        ),
    )
    zz = 512 + brick * 8 + r + jnp.where(side > 4.5, 64, 0)
    return jnp.where(side < 3.5, xy, zz)


def shift_rows(v, amount):
    return pltpu.roll(v, amount % v.shape[0], 0)


def z_table(v, mask, select):
    i, j = iota((128, LANES), 0), iota((128, LANES), 1)
    low = one_hot(i == (j & 63))
    high = one_hot(i - 64 == (j & 63))
    first = jnp.where(mask, dot(v[:, 0:128], low), 0.0).astype(BF16)
    last = jnp.where(mask, dot(v[:, 384:512], high), 0.0).astype(BF16)
    return dot(select, first).astype(BF16), dot(select, last).astype(BF16)


def diagonal_sum(blocks, low_shift, high_shift, count):
    even = odd = None
    for z in range(count):
        zr, zc = z + low_shift, z + high_shift
        if not (0 <= zr < count and 0 <= zc < count):
            continue
        piece = blocks[64 * zr : 64 * zr + 64, 128 * (zc // 2) : 128 * (zc // 2) + 128]
        if zc % 2 == 0:
            even = piece if even is None else even + piece
        else:
            odd = piece if odd is None else odd + piece
    return even + pltpu.roll(odd, 64, 1)


def kernel(
    n_grp,
    n_dev,
    features_ref,
    cotangent_ref,
    steps_ref,
    links_ref,
    sources_ref,
    targets_ref,
    places_ref,
    time_weight_ref,
    fine_weight_ref,
    down_weight_ref,
    coarse_weight_ref,
    up_weight_ref,
    frequency_ref,
    mixed_ref,
    input_grad_ref,
    fine_grad_ref,
    down_grad_ref,
    coarse_grad_ref,
    up_grad_ref,
    time_grad_ref,
    small_out,
    small_in,
    face_out,
    face_in,
    rim_out,
    rim_in,
    back_out,
    back_in,
    part_out,
    part_in,
    unit_out,
    unit_in,
    sum_out,
    sum_in,
    whole,
    time_out,
    time_in,
    time_mid,
    time_whole,
    hot_halo,
    hot_out,
    table,
    normed_ref,
    slope_ref,
    conv_ref,
    grad_ref,
    weight_ref,
    band_ref,
    send_sems,
    recv_sems,
):
    grp = lax.axis_index("grp")
    dev = lax.axis_index("dev")
    units = UNITS
    unit_rows = PART_ROWS // n_grp // units
    owners = min(n_grp, 8)
    owner_rows = 64 // owners

    def entry_signal():
        barrier = pltpu.get_barrier_semaphore()

        def to_dev(j, carry):
            pl.semaphore_signal(
                barrier,
                inc=1,
                device_id={"grp": grp, "dev": lax.rem(dev + j, n_dev)},
                device_id_type=pl.DeviceIdType.MESH,
            )
            return carry

        def to_grp(j, carry):
            pl.semaphore_signal(
                barrier,
                inc=1,
                device_id={"grp": lax.rem(grp + j, n_grp), "dev": dev},
                device_id_type=pl.DeviceIdType.MESH,
            )
            return carry

        lax.fori_loop(1, n_dev, to_dev, 0)
        lax.fori_loop(1, n_grp, to_grp, 0)

    def remote(src, dst, index, along, peer):
        target = {"grp": grp, "dev": peer} if along == "dev" else {"grp": peer, "dev": dev}
        return pltpu.make_async_remote_copy(
            src_ref=src,
            dst_ref=dst,
            send_sem=send_sems.at[index],
            recv_sem=recv_sems.at[index],
            device_id=target,
            device_id_type=pl.DeviceIdType.MESH,
        )

    def position(along):
        return (dev, n_dev) if along == "dev" else (grp, n_grp)

    def exchange(src, dst, index, along):
        me, count = position(along)

        def step(j, carry):
            p = lax.rem(me + j, count)
            remote(src.at[p], dst.at[me], index, along, p).start()
            return carry

        lax.fori_loop(1, count, step, 0)

    def wait_arrived(dst, blocks, index, along):
        me, count = position(along)
        if blocks > 0:
            part = dst.at[pl.ds(0, blocks)]
            remote(part, part, index, along, lax.rem(me + 1, count)).wait_recv()

    def wait_sent(src, blocks, index, along):
        me, count = position(along)
        if blocks > 0:
            part = src.at[pl.ds(0, blocks)]
            remote(part, part, index, along, lax.rem(me + 1, count)).wait_send()

    entry_signal()

    row = iota((ROWS, LANES), 0)
    lane = iota((ROWS, LANES), 1)
    y_mask = (lane >> 6) == (row & 7)

    def spread_index(shape):
        return iota(shape, 0), iota(shape, 1)

    i, j = spread_index((n_dev, n_dev * SLOT_ROWS))
    sources = sources_ref[0].astype(F32)
    chosen = jnp.where(((j >> 3) & 1) == 0, sources[:, 0:1], sources[:, 1:2])
    code = jnp.sum(jnp.where((j >> 4) == i, chosen, 0.0), axis=0, keepdims=True)
    brick = jnp.zeros_like(code)
    for m in range(1, BRICKS):
        brick = brick + jnp.where(code > 6.0 * m - 0.5, 1.0, 0.0)
    r = (iota(code.shape, 1) & 7).astype(F32)
    out_index = jnp.where(code < -0.5, -1.0, face_index(brick, code - 6.0 * brick, r))
    out_index = out_index.astype(jnp.int32)
    hot_out[...] = one_hot(iota((640, n_dev * SLOT_ROWS), 0) == out_index)

    i, j = spread_index((BRICKS, 384))
    links = links_ref[...].astype(F32)
    link = jnp.zeros((BRICKS, 384), F32)
    for k in range(6):
        link = link + jnp.where((j >> 6) == k, links[:, k : k + 1], 0.0)
    link = jnp.sum(jnp.where(((j >> 3) & 7) == i, link, 0.0), axis=0, keepdims=True)
    k_row = iota((1, 384), 1) >> 6
    side = (k_row + 1 - 2 * (k_row & 1)).astype(F32)
    r = (iota((1, 384), 1) & 7).astype(F32)
    halo_index = jnp.where(
        link < -0.5,
        -1.0,
        jnp.where(link < 7.5, face_index(link, side, r), 640 + (link - 8.0) * 8 + r),
    ).astype(jnp.int32)
    hot_halo[...] = one_hot(iota((640 + n_dev * SLOT_ROWS, 384), 0) == halo_index)

    i, j = spread_index((64, BRICKS))
    targets = targets_ref[...].astype(F32).reshape(1, BRICKS)
    target = jnp.sum(jnp.where((i >> 3) == j, targets, 0.0), axis=1, keepdims=True)
    child = (iota((64, 1), 0) & 7).astype(F32)
    target_code = (target * 16 + child).astype(jnp.int32)
    slot_lane = iota((64, n_dev * SLOT_ROWS), 1)
    hot_target = one_hot(slot_lane == target_code)
    hot_target_grad = one_hot(slot_lane == target_code + 8)

    i, j = spread_index((64, ROWS))
    pool = one_hot(
        ((i >> 3) == (j >> 6))
        & (((i >> 2) & 1) == ((j >> 5) & 1))
        & (((i >> 1) & 1) == ((j >> 2) & 1))
    )
    i, j = spread_index((64, LANES))
    half_mask = (i & 1) == (j >> 8)
    select_x = one_hot(i == (j >> 3))
    i, j = spread_index((ROWS, 64))
    unpool = one_hot(
        ((j >> 3) == (i >> 6))
        & (((j >> 2) & 1) == ((i >> 5) & 1))
        & (((j >> 1) & 1) == ((i >> 2) & 1))
    )
    repeat_y = one_hot(j == (i >> 3))
    repeat_x = one_hot(j == ((i >> 6) * 8 + (i & 7)))
    low_half = iota((64, 128), 1) < 64

    features = features_ref[...].astype(F32).reshape(ROWS, LANES)
    f3 = features.reshape(BRICKS, 64, LANES)
    centred = f3 - per_brick(group_mean(jnp.sum(f3, axis=1)))
    variance = group_mean(jnp.sum(centred * centred, axis=1))
    inverse = lax.rsqrt(variance + EPSILON)
    normed = (centred * per_brick(inverse)).reshape(ROWS, LANES)
    normed_ref[...] = normed
    i, j = spread_index((BRICKS, BRICKS))
    steps = steps_ref[...].astype(F32).reshape(1, BRICKS)
    step_column = jnp.sum(jnp.where(i == j, steps, 0.0), axis=1, keepdims=True)
    angles = step_column * frequency_ref[...]
    embedding = jnp.where(iota((BRICKS, 64), 1) < 32, jnp.cos(angles), jnp.sin(angles))
    modulate = jnp.dot(
        embedding,
        time_weight_ref[...],
        precision=lax.Precision.HIGHEST,
        preferred_element_type=F32,
    )
    swapped = pltpu.roll(modulate, 64, 1)
    low_b = iota((BRICKS, 128), 1) < 64
    scale = lanes_four(jnp.where(low_b, modulate, swapped))
    shift = lanes_four(jnp.where(low_b, swapped, modulate))
    gain = 1.0 + scale
    before = (
        normed.reshape(BRICKS, 64, LANES) * per_brick(gain) + per_brick(shift)
    ).reshape(ROWS, LANES)
    sigmoid = 1.0 / (1.0 + jnp.exp(-before))
    slope_ref[...] = sigmoid * (1.0 + before * (1.0 - sigmoid))
    active = (before * sigmoid).astype(BF16)
    table[0:512, :] = active

    grad = cotangent_ref[...].astype(F32).reshape(ROWS, LANES)
    grad_b = grad.astype(BF16)
    pooled = fold_lanes(jnp.where(half_mask, dot(pool, active), 0.0)) * (1.0 / 64.0)
    grad_up = fold_lanes(jnp.where(half_mask, dot(pool, grad_b), 0.0))
    small = jnp.where(low_half, pooled, grad_up).astype(BF16)
    small_out[...] = dot_tn(hot_target, small).astype(BF16).reshape(n_dev, SLOT_ROWS, 128)
    small_in[dev] = small_out[dev]
    barrier = pltpu.get_barrier_semaphore()
    pl.semaphore_wait(barrier, n_dev - 1 + n_grp - 1)
    exchange(small_out, small_in, 0, "dev")

    z_first, z_last = z_table(active, y_mask, select_x)
    table[512:576, :] = z_first
    table[576:640, :] = z_last
    face_out[...] = (
        dot_tn(hot_out[...], table[...]).astype(BF16).reshape(n_dev, SLOT_ROWS, LANES)
    )
    face_in[dev] = face_out[dev]
    exchange(face_out, face_in, 1, "dev")

    i, j = spread_index((64, LANES))
    wide = dot(fine_weight_ref[...].reshape(448, 64), one_hot(i == (j & 63)))
    weight_ref[...] = wide
    i, j = spread_index((256, 256))
    block = (i >> 6) == (j >> 6)
    for k in range(6):
        piece = weight_ref[64 * (k + 1) : 64 * (k + 2), 0:256]
        band_ref[256 * k : 256 * (k + 1), :] = jnp.where(
            block, jnp.concatenate([piece] * 4, axis=0), 0.0
        ).astype(BF16)
    z_step = (lane >> 6) - (row >> 6)
    middle = jnp.where(
        z_step == 0,
        jnp.concatenate([weight_ref[0:64, :]] * 8, axis=0),
        jnp.where(
            z_step == 1,
            jnp.concatenate([weight_ref[320:384, :]] * 8, axis=0),
            jnp.where(
                z_step == -1, jnp.concatenate([weight_ref[384:448, :]] * 8, axis=0), 0.0
            ),
        ),
    ).astype(BF16)

    i, j = spread_index((64, ROWS))
    g4 = grad.reshape(BRICKS, 8, 8, LANES)
    grad_z = z_table(grad_b, y_mask, select_x)
    layers = [
        g4[:, 0].reshape(64, LANES).astype(BF16),
        g4[:, 7].reshape(64, LANES).astype(BF16),
        dot(one_hot(j == i * 8), grad_b).astype(BF16),
        dot(one_hot(j == i * 8 + 7), grad_b).astype(BF16),
        grad_z[0],
        grad_z[1],
    ]
    rims = []
    for k in range(6):
        band = band_ref[256 * k : 256 * (k + 1), :]
        rims.append(
            jnp.concatenate(
                [dot_nt(layers[k][:, 0:256], band), dot_nt(layers[k][:, 256:512], band)], axis=1
            ).astype(BF16)
        )
    rim = jnp.concatenate(rims, axis=0)
    rim_out[...] = (
        dot(hot_halo[640 : 640 + n_dev * SLOT_ROWS, :], rim)
        .astype(BF16)
        .reshape(n_dev, SLOT_ROWS, LANES)
    )
    rim_in[dev] = rim_out[dev]
    exchange(rim_out, rim_in, 2, "dev")

    x_at, y_at = (row >> 3) & 7, row & 7

    def shifted(v, k, edge):
        amount, at, end = ((8, x_at, 0), (-8, x_at, 7), (1, y_at, 0), (-1, y_at, 7))[k]
        return jnp.where(at == end, edge, shift_rows(v, amount))

    total = dot_nt(grad_b, middle)
    left, right = total[:, 0:256], total[:, 256:512]
    for k in range(4):
        moved = shifted(grad, k ^ 1, 0.0).astype(BF16)
        band = band_ref[256 * k : 256 * (k + 1), :]
        left = left + dot_nt(moved[:, 0:256], band)
        right = right + dot_nt(moved[:, 256:512], band)
    total = jnp.concatenate([left, right], axis=1)
    total = total + dot(hot_halo[0:512, :], rim)
    z_rows = dot(hot_halo[512:640, :], rim)
    grad_ref[...] = total

    active_f = active.astype(F32)
    conv_ref[...] = dot(active, middle)
    grad_t = grad.T.astype(BF16)
    center = dot(grad_t, active)

    wait_arrived(small_in, n_dev - 1, 0, "dev")
    i, j = spread_index((n_dev, n_dev * SLOT_ROWS))
    places = places_ref[0].astype(F32)
    place = jnp.sum(jnp.where((j >> 4) == i, places, 0.0), axis=0, keepdims=True)
    j = iota((1, n_dev * SLOT_ROWS), 1)
    place_code = (place * 8 + (j & 7).astype(F32)).astype(jnp.int32)
    i = iota((ROWS, 1), 0)
    voxel_code = (
        ((i >> 7) * 16 + ((i >> 4) & 3) * 4 + ((i >> 1) & 3)) * 8
        + ((i >> 6) & 1) * 4
        + ((i >> 3) & 1) * 2
        + (i & 1)
    )
    first_kind = (j & 8) == 0
    hot_place = one_hot(voxel_code == jnp.where(first_kind, place_code, -1))
    hot_place_grad = one_hot(voxel_code == jnp.where(first_kind, -1, place_code))
    grid = dot(hot_place, small_in[...].reshape(n_dev * SLOT_ROWS, 128)).astype(BF16)
    down = jnp.concatenate([down_weight_ref[...], jnp.zeros((64, 128), BF16)], axis=0)
    i, j = spread_index((64, 128))
    up = dot(up_weight_ref[...], one_hot(j - 64 == i)).astype(BF16)
    coarse_pre = dot(grid, down)
    coarse_sig = 1.0 / (1.0 + jnp.exp(-coarse_pre))
    coarse_act = coarse_pre * coarse_sig
    row_c = iota((ROWS, 128), 0)
    at_c = (row_c >> 6, (row_c >> 3) & 7, row_c & 7)

    def coarse_shifted(v, k):
        amount = (64, -64, 8, -8, 1, -1)[k]
        return jnp.where(at_c[k // 2] == 7 * (k % 2), 0.0, shift_rows(v, amount))

    coarse_act_f = coarse_act.astype(BF16).astype(F32)
    stack = jnp.concatenate(
        [coarse_act_f.astype(BF16)]
        + [coarse_shifted(coarse_act_f, k).astype(BF16) for k in range(6)],
        axis=1,
    )
    coarse_out = dot(stack, coarse_weight_ref[...].reshape(896, 128)).astype(BF16)
    grad_out = dot_nt(grid, up)
    grad_out_b = grad_out.astype(BF16)
    grad_act = dot_nt(grad_out_b, coarse_weight_ref[0])
    for k in range(6):
        grad_act = grad_act + dot_nt(
            coarse_shifted(grad_out, k ^ 1).astype(BF16), coarse_weight_ref[k + 1]
        )
    grad_pre = grad_act * coarse_sig * (1.0 + coarse_pre * (1.0 - coarse_sig))
    grad_pre = grad_pre.astype(BF16)
    grad_pooled = dot_nt(grad_pre, down).astype(BF16)
    back_out[...] = (
        (dot_tn(hot_place, coarse_out) + dot_tn(hot_place_grad, grad_pooled))
        .astype(BF16)
        .reshape(n_dev, SLOT_ROWS, 128)
    )
    back_in[dev] = back_out[dev]
    exchange(back_out, back_in, 3, "dev")
    coarse_grad = dot_tn(stack, grad_out_b)
    down_grad = dot_tn(grid, grad_pre)
    up_grad = dot_tn(coarse_out, grid)
    up_rows = jnp.where(low_half, pltpu.roll(up_grad[0:64], 64, 1), up_grad[64:128])

    wait_arrived(face_in, n_dev - 1, 1, "dev")
    halo = dot_tn(hot_halo[0:640, :], table[...]) + dot_tn(
        hot_halo[640 : 640 + n_dev * SLOT_ROWS, :],
        face_in[...].reshape(n_dev * SLOT_ROWS, LANES),
    )
    halo = halo.astype(BF16)
    tap_grads = [diagonal_sum(center, 0, 0, 8)]
    conv = conv_ref[...]
    left, right = conv[:, 0:256], conv[:, 256:512]
    for k in range(4):
        repeat = repeat_x if k < 2 else repeat_y
        moved = shifted(active_f, k, dot(repeat, halo[64 * k : 64 * k + 64])).astype(BF16)
        band = band_ref[256 * k : 256 * (k + 1), :]
        left = left + dot(moved[:, 0:256], band)
        right = right + dot(moved[:, 256:512], band)
        tap_grads.append(
            diagonal_sum(dot(grad_t[0:256], moved[:, 0:256]), 0, 0, 4)
            + diagonal_sum(dot(grad_t[256:512], moved[:, 256:512]), 0, 0, 4)
        )
    layer = jnp.where(y_mask, dot(repeat_y, halo[256:320]), 0.0).astype(BF16)
    tail = jnp.concatenate(
        [jnp.where(low_half, weight_ref[320:384, 0:128], 0.0).astype(BF16)] * 8, axis=0
    )
    left = jnp.concatenate([left[:, 0:128] + dot(layer, tail), left[:, 128:256]], axis=1)
    tap_grads.append(
        diagonal_sum(center, 0, -1, 8) + fold_lanes(dot(grad_t[0:64], layer))
    )
    layer = jnp.where(y_mask, dot(repeat_y, halo[320:384]), 0.0).astype(BF16)
    tail = jnp.concatenate(
        [jnp.where(low_half, 0.0, weight_ref[384:448, 0:128]).astype(BF16)] * 8, axis=0
    )
    right = jnp.concatenate([right[:, 0:128], right[:, 128:256] + dot(layer, tail)], axis=1)
    tap_grads.append(
        diagonal_sum(center, 0, 1, 8) + fold_lanes(dot(grad_t[448:512], layer))
    )
    conv_ref[...] = jnp.concatenate([left, right], axis=1)

    fine_rows = []
    for t in range(4):
        low = tap_grads[t].T[0:64]
        high = tap_grads[t + 4].T[0:64] if t < 3 else jnp.zeros_like(low)
        fine_rows.append(jnp.concatenate([low, high], axis=1))
    part = jnp.concatenate([coarse_grad, down_grad[0:64], up_rows] + fine_rows, axis=0)
    part_out[...] = part.astype(BF16).reshape(n_grp, PART_ROWS // n_grp, 128)
    part_in[grp] = part_out[grp]
    exchange(part_out, part_in, 4, "grp")

    wait_arrived(back_in, n_dev - 1, 3, "dev")
    back = back_in[...].reshape(n_dev * SLOT_ROWS, 128)
    coarse_values = dot(hot_target, back).astype(BF16)
    i, j = spread_index((64, LANES))
    up_wide = dot(up_weight_ref[...], one_hot(i == (j & 63))).astype(BF16)
    upward = jnp.where(half_mask, dot(coarse_values, up_wide), 0.0)
    upward_high = upward.astype(BF16)
    upward_low = (upward - upward_high.astype(F32)).astype(BF16)
    upward = dot(unpool, upward_high) + dot(unpool, upward_low)
    features = features_ref[...].astype(F32).reshape(ROWS, LANES)
    mixed = features + conv_ref[...] + upward
    mixed_ref[...] = mixed.reshape(BRICKS, 8, 8, LANES).astype(BF16)

    wait_arrived(part_in, n_grp - 1, 4, "grp")
    own = part_in[0].astype(F32)
    for p in range(1, n_grp):
        own = own + part_in[p].astype(F32)
    unit_out[...] = own.reshape(units, unit_rows, 128)

    def to_owner(j, carry):
        p = lax.rem(dev + j, n_dev)

        @pl.when(p < units)
        def _():
            remote(unit_out.at[p], unit_in.at[dev], 5, "dev", p).start()

        return carry

    lax.fori_loop(1, n_dev, to_owner, 0)

    back_grad = dot(hot_target_grad, back).astype(BF16)
    i, j = spread_index((128, LANES))
    back_wide = jnp.where(half_mask, dot(back_grad, one_hot(i == (j & 63))), 0.0)
    total = grad_ref[...] + dot(unpool, (back_wide * (1.0 / 64.0)).astype(BF16))
    wait_arrived(rim_in, n_dev - 1, 2, "dev")
    rim_back = rim_in[...].reshape(n_dev * SLOT_ROWS, LANES)
    total = total + dot(hot_out[0:512, :], rim_back)
    z_rows = (z_rows + dot(hot_out[512:640, :], rim_back)).astype(BF16)
    low_rows = lane[:, 0:128] < 64
    first = fold_lanes(jnp.where(y_mask, dot(repeat_y, z_rows[0:64]), 0.0))
    last = fold_lanes(jnp.where(y_mask, dot(repeat_y, z_rows[64:128]), 0.0))
    total = jnp.concatenate(
        [
            total[:, 0:128] + jnp.where(low_rows, first, 0.0),
            total[:, 128:384],
            total[:, 384:512] + jnp.where(low_rows, 0.0, last),
        ],
        axis=1,
    )
    normed = normed_ref[...]
    grad_before = total * slope_ref[...]
    grad_scale = fold_lanes(brick_sum(grad_before * normed))
    grad_shift = fold_lanes(brick_sum(grad_before))
    time_grad = lax.dot_general(
        embedding,
        jnp.where(low_b, grad_scale, grad_shift),
        (((0,), (0,)), ((), ())),
        precision=lax.Precision.HIGHEST,
        preferred_element_type=F32,
    )
    time_out[...] = time_grad.reshape(owners, owner_rows, 128)

    def to_time_owner(j, carry):
        p = lax.rem(grp + j, n_grp)

        @pl.when(p < owners)
        def _():
            remote(time_out.at[p], time_in.at[grp], 8, "grp", p).start()

        return carry

    lax.fori_loop(1, n_grp, to_time_owner, 0)

    @pl.when(dev < units)
    def _():
        unit_in[dev] = unit_out[dev]
        wait_arrived(unit_in, n_dev - 1, 5, "dev")
        mine = unit_in[0]
        for p in range(1, n_dev):
            mine = mine + unit_in[p]
        sum_out[...] = mine
        sum_in[dev] = mine

        def to_all(j, carry):
            p = lax.rem(dev + j, n_dev)
            remote(sum_out, sum_in.at[dev], 6, "dev", p).start()
            return carry

        lax.fori_loop(1, n_dev, to_all, 0)

    g3 = grad_before.reshape(BRICKS, 64, LANES) * per_brick(gain)
    n3 = normed.reshape(BRICKS, 64, LANES)
    mean_g = group_mean(jnp.sum(g3, axis=1))
    mean_gn = group_mean(jnp.sum(g3 * n3, axis=1))
    result = per_brick(inverse) * (g3 - per_brick(mean_g) - n3 * per_brick(mean_gn))
    grad = cotangent_ref[...].astype(F32).reshape(ROWS, LANES)
    result = grad + result.reshape(ROWS, LANES)
    input_grad_ref[...] = result.reshape(BRICKS, 8, 8, LANES).astype(BF16)

    @pl.when(grp < owners)
    def _():
        time_in[grp] = time_out[grp]
        wait_arrived(time_in, n_grp - 1, 8, "grp")
        mine = time_in[0]
        for p in range(1, n_grp):
            mine = mine + time_in[p]
        time_mid[dev] = mine

        def to_all(j, carry):
            p = lax.rem(dev + j, n_dev)
            remote(time_mid.at[dev], time_mid.at[dev], 9, "dev", p).start()
            return carry

        lax.fori_loop(1, n_dev, to_all, 0)

    @pl.when(dev < units)
    def _():
        wait_arrived(sum_in, units - 1, 6, "dev")

    @pl.when(dev >= units)
    def _():
        wait_arrived(sum_in, units, 6, "dev")

    whole[grp] = sum_in[...].reshape(units * unit_rows, 128).astype(BF16)

    def to_all(j, carry):
        p = lax.rem(grp + j, n_grp)
        remote(whole.at[grp], whole.at[grp], 7, "grp", p).start()
        return carry

    lax.fori_loop(1, n_grp, to_all, 0)

    @pl.when(grp < owners)
    def _():
        wait_arrived(time_mid, n_dev - 1, 9, "dev")
        mine = time_mid[0]
        for p in range(1, n_dev):
            mine = mine + time_mid[p]
        time_whole[grp] = mine

        def to_all(j, carry):
            p = lax.rem(grp + j, n_grp)
            remote(time_whole.at[grp], time_whole.at[grp], 10, "grp", p).start()
            return carry

        lax.fori_loop(1, n_grp, to_all, 0)

    wait_arrived(whole, n_grp - 1, 7, "grp")
    sums = whole[...].reshape(PART_ROWS, 128).astype(F32)
    coarse_grad_ref[...] = sums[0:896].reshape(7, 128, 128)
    down_grad_ref[...] = sums[896:960]
    up_grad_ref[0:64, :] = sums[960:1024, 0:64]
    up_grad_ref[64:128, :] = pltpu.roll(sums[960:1024], 64, 1)[:, 0:64]
    for t in range(4):
        piece = sums[1024 + 64 * t : 1088 + 64 * t]
        fine_grad_ref[t] = piece[:, 0:64]
        if t < 3:
            fine_grad_ref[t + 4] = pltpu.roll(piece, 64, 1)[:, 0:64]

    @pl.when(grp < owners)
    def _():
        wait_arrived(time_whole, owners - 1, 10, "grp")

    @pl.when(grp >= owners)
    def _():
        wait_arrived(time_whole, owners, 10, "grp")

    time_grad_ref[...] = time_whole[...].reshape(64, 128)

    wait_sent(small_out, n_dev - 1, 0, "dev")
    wait_sent(face_out, n_dev - 1, 1, "dev")
    wait_sent(rim_out, n_dev - 1, 2, "dev")
    wait_sent(back_out, n_dev - 1, 3, "dev")
    wait_sent(part_out, n_grp - 1, 4, "grp")
    wait_sent(whole, n_grp - 1, 7, "grp")

    @pl.when(dev < units)
    def _():
        wait_sent(unit_out, units - 1, 5, "dev")
        wait_sent(unit_in, n_dev - 1, 6, "dev")

    @pl.when(dev >= units)
    def _():
        wait_sent(unit_out, units, 5, "dev")

    @pl.when(grp < owners)
    def _():
        wait_sent(time_out, owners - 1, 8, "grp")
        wait_sent(time_mid, n_dev - 1, 9, "dev")
        wait_sent(time_in, n_grp - 1, 10, "grp")

    @pl.when(grp >= owners)
    def _():
        wait_sent(time_out, owners, 8, "grp")


def body(n_grp, n_dev, *args):
    half = 32
    frequency = np.exp(-math.log(10000.0) * np.arange(half) / half).astype(np.float32)
    frequency = jnp.asarray(np.concatenate([frequency, frequency])[None, :])
    chunk = PART_ROWS // n_grp
    units, unit_rows = UNITS, chunk // UNITS
    owners = min(n_grp, 8)
    owner_rows = 64 // owners
    vmem = pl.BlockSpec(memory_space=pltpu.VMEM)
    packed = jax.ShapeDtypeStruct((BRICKS, 8, 8, LANES), BF16)
    slots = (n_dev, SLOT_ROWS)
    return pl.pallas_call(
        functools.partial(kernel, n_grp, n_dev),
        out_shape=(
            packed,
            packed,
            jax.ShapeDtypeStruct((7, 64, 64), F32),
            jax.ShapeDtypeStruct((64, 128), F32),
            jax.ShapeDtypeStruct((7, 128, 128), F32),
            jax.ShapeDtypeStruct((128, 64), F32),
            jax.ShapeDtypeStruct((64, 128), F32),
        ),
        in_specs=[vmem] * 13,
        out_specs=(vmem,) * 7,
        scratch_shapes=[
            pltpu.VMEM(slots + (128,), BF16),
            pltpu.VMEM(slots + (128,), BF16),
            pltpu.VMEM(slots + (LANES,), BF16),
            pltpu.VMEM(slots + (LANES,), BF16),
            pltpu.VMEM(slots + (LANES,), BF16),
            pltpu.VMEM(slots + (LANES,), BF16),
            pltpu.VMEM(slots + (128,), BF16),
            pltpu.VMEM(slots + (128,), BF16),
            pltpu.VMEM((n_grp, chunk, 128), BF16),
            pltpu.VMEM((n_grp, chunk, 128), BF16),
            pltpu.VMEM((units, unit_rows, 128), F32),
            pltpu.VMEM((n_dev, unit_rows, 128), F32),
            pltpu.VMEM((unit_rows, 128), F32),
            pltpu.VMEM((units, unit_rows, 128), F32),
            pltpu.VMEM((n_grp, chunk, 128), BF16),
            pltpu.VMEM((owners, owner_rows, 128), F32),
            pltpu.VMEM((n_grp, owner_rows, 128), F32),
            pltpu.VMEM((n_dev, owner_rows, 128), F32),
            pltpu.VMEM((owners, owner_rows, 128), F32),
            pltpu.VMEM((640 + n_dev * SLOT_ROWS, 384), BF16),
            pltpu.VMEM((640, n_dev * SLOT_ROWS), BF16),
            pltpu.VMEM((640, LANES), BF16),
            pltpu.VMEM((ROWS, LANES), F32),
            pltpu.VMEM((ROWS, LANES), F32),
            pltpu.VMEM((ROWS, LANES), F32),
            pltpu.VMEM((ROWS, LANES), F32),
            pltpu.VMEM((448, LANES), F32),
            pltpu.VMEM((1536, 256), BF16),
            pltpu.SemaphoreType.DMA((11,)),
            pltpu.SemaphoreType.DMA((11,)),
        ],
        compiler_params=pltpu.CompilerParams(
            collective_id=0, has_side_effects=True, vmem_limit_bytes=56 * 1024 * 1024
        ),
    )(*args, frequency)


def solution(mesh):
    split = ("grp", "dev")
    in_specs = (
        P(split, None, None, None),
        P(split, None, None, None),
        P(split),
        P(split, None),
        P(split, None, None),
        P(split),
        P(split, None, None),
        P(),
        P(),
        P(),
        P(),
        P(),
    )
    out_specs = (
        P(split, None, None, None),
        P(split, None, None, None),
        P(),
        P(),
        P(),
        P(),
        P(),
    )
    return jax.shard_map(
        functools.partial(body, mesh.shape["grp"], mesh.shape["dev"]),
        mesh=mesh,
        in_specs=in_specs,
        out_specs=out_specs,
        check_vma=False,
    )
```

time: 819 us -> 63.6 us (0.08); the launches traced: 807 us -> 63.3 us
  waiting for transfers between devices: 456 us -> 0 us
  local copies, waits for them, and re-layouts: 200 us -> 10.7 us
  other arithmetic: 63.5 us -> 0 us
  Pallas kernels: 0 us -> 52 us
  starting transfers between devices: 39.8 us -> 0 us
  matrix products: 32.2 us -> 0 us
  between operations: 15.7 us -> 0.66 us
    psum x2 -> x0, waiting for transfers between devices: 436 us -> none  [body(): lax.psum((fine_grad, down_grad, coarse_grad, up_grad, time_grad), ('grp',...]
    pallas_call x0 -> x1, Pallas kernels: none -> 52 us  [body(): pl.pallas_call(functools.partial(kernel, n_grp, n_dev), out_shape=(packed...]
    scatter x31 -> x0, local copies, waits for them, and re-layouts: 47.5 us -> none  [the longest x4 15 us: padded_volume(): padded = padded.at[:, 1:9, 1:9, 9].set(layers[:, 5])]
    all_to_all x6 -> x0, starting transfers between devices: 39.5 us -> none  [the longest x1 9.98 us: body(): lax.all_to_all(pooled_out, 'dev', split_axis=0, concat_axis=0, tiled=True)]
    dot_general x20 -> x0, matrix products: 32.2 us -> none  [the longest x6 7.98 us: rim_gradients(): jnp.dot(grad_layer, fine_weight[direction + 1].T, preferred_element_type=...]
    reduce_sum x7 -> x0, other arithmetic: 31.6 us -> none  [the longest x1 13.5 us: activate(): jnp.mean(jnp.square(grouped - centre_mean), axis=(1, 3), keepdims=True)]
    concatenate x13 -> x0, local copies, waits for them, and re-layouts: 23.1 us -> none  [the longest x4 19.8 us: tap_stack(): return jnp.concatenate(pieces, axis=-1)]
    another operation x31 -> x0, local copies, waits for them, and re-layouts: 22 us -> none  [the longest x8 12.4 us: rim_gradients(): return jnp.stack(rim_list, axis=1).reshape(brick_count * 6, 8, 8 * channels)]
  transfers between devices with their start and end apart: 8 -> 0, of which waited for: 6 -> 0; matrix products, arithmetic and copies ran while one was open for 21% -> 0% of each run, Pallas kernels for 0% -> 0%
where the time goes in v1:
time: 63.6 us; the launch traced here: 63.3 us
  Pallas kernels  52 us (82%)
  local copies, waits for them, and re-layouts  10.7 us (17%)
  between operations  0.66 us (1%)
    pallas_call x1, Pallas kernels, body(): pl.pallas_call(functools.partial(kernel, n_grp, n_dev), out_shape=(packed...  52 us
    unnamed x21, local copies, waits for them, and re-layouts  9.16 us
    pallas_call x1, local copies, waits for them, and re-layouts, body(): pl.pallas_call(functools.partial(kernel, n_grp, n_dev), out_shape=(packed...  1.54 us

profile of v1, /device:TPU:1, one launch (start us, length us, event | category | flops | bytes accessed | tf_op | source)
XLA Modules:
  0.0 63.3 jit_solution(3797964845686834007)
XLA Ops:
  0.6 0.0 copy-start.5
  0.6 1.4 %copy.20.sources_ref = s32[1,16,2]{2,1,0:T(8,128)} copy(s32[1,16,2]{1,2,0:T(2,128)} %param.17) | data formatting | bytes 256 | tf_op args[4]
  2.0 1.3 %copy.21.places_ref = s32[1,16,1]{2,1,0:T(8,128)} copy(s32[1,16,1]{1,2,0:T(1,128)} %param.19) | data formatting | bytes 128 | tf_op args[6]
  3.3 0.0 copy-done.5
  3.3 0.7 %copy.22.up_weight_ref = bf16[128,64]{1,0:T(8,128)(2,1)} copy(bf16[128,64]{0,1:T(8,128)(2,1)S(1)} %copy-done.5) | data formatting | bytes 32768 | tf_op args[11]
  4.1 52.0 %shard_map.180 = (bf16[8,8,8,512]{3,2,1,0:T(8,128)(2,1)}, bf16[8,8,8,512]{3,2,1,0:T(8,128)(2,1)}, f32[7,64,64]{2,1,0:T(8,128)}, f32[64,128]{1,0:T(8,128)}, f32[7...) custom-call(bf16[8,8,8,512]{3,2,1,0:T(8,128)(2,1)} %features_ref.1, bf16[8,8,8,512]{3,2,1,0:T(8,128)(2,1)} %cotangent_ref.1, ...), custom_call_target="tpu_custom_call" | custom-call | tf_op jit(solution)/shard_map/pallas_call | solution.py:733
  56.0 1.5 %copy.23 = f32[128,64]{0,1:T(8,128)} copy(f32[128,64]{1,0:T(8,128)} %get-tuple-element.12) | data formatting | bytes 65536 | tf_op jit(solution)/shard_map/pallas_call | solution.py:733
  57.6 0.0 copy-start
  57.6 1.9 %copy.30 = bf16[8,8,8,512]{3,2,1,0:T(8,128)(2,1)} copy(bf16[8,8,8,512]{3,2,1,0:T(8,128)(2,1)} %get-tuple-element.21) | data formatting | bytes 1048576
  59.5 0.0 copy-done
  59.5 0.0 copy-start.2
  59.5 0.0 copy-start.4
  59.5 0.8 %copy.31 = bf16[8,8,8,512]{3,2,1,0:T(8,128)(2,1)} copy(bf16[8,8,8,512]{3,2,1,0:T(8,128)(2,1)S(1)} %copy-done) | data formatting | bytes 1048576
  60.3 0.3 copy-done.2
  60.6 0.0 copy-start.1
  60.6 0.7 %copy.32 = f32[7,64,64]{2,1,0:T(8,128)} copy(f32[7,64,64]{2,1,0:T(8,128)S(1)} %copy-done.2) | data formatting | bytes 229376
  61.3 0.0 copy-done.4
  61.3 0.6 copy.33
  61.9 0.0 copy-done.1
  61.9 0.0 copy-start.3
  62.0 0.8 %copy.34 = f32[7,128,128]{2,1,0:T(8,128)} copy(f32[7,128,128]{2,1,0:T(8,128)S(1)} %copy-done.1) | data formatting | bytes 917504
  62.7 0.0 copy-done.3
  62.7 0.6 copy.35
Async XLA Ops:
  0.6 2.7 %copy-start.5 = (bf16[128,64]{0,1:T(8,128)(2,1)S(1)}, bf16[128,64]{0,1:T(8,128)(2,1)}, u32[]{:S(2)}) copy-start(bf16[128,64]{0,1:T(8,128)(2,1)} %param.24) | copy-start | bytes 49156
  57.6 1.9 %copy-start = (bf16[8,8,8,512]{3,2,1,0:T(8,128)(2,1)S(1)}, bf16[8,8,8,512]{3,2,1,0:T(8,128)(2,1)}, u32[]{:S(2)}) copy-start(bf16[8,8,8,512]{3,2,1,0:T(8,128)(2,1)} %get-tuple-element.22) | copy-start | bytes 1572868
  59.5 1.1 %copy-start.2 = (f32[7,64,64]{2,1,0:T(8,128)S(1)}, f32[7,64,64]{2,1,0:T(8,128)}, u32[]{:S(2)}) copy-start(f32[7,64,64]{2,1,0:T(8,128)} %get-tuple-element.23) | copy-start | bytes 344068
  59.5 1.8 %copy-start.4 = (f32[64,128]{1,0:T(8,128)S(1)}, f32[64,128]{1,0:T(8,128)}, u32[]{:S(2)}) copy-start(f32[64,128]{1,0:T(8,128)} %get-tuple-element.24) | copy-start | bytes 98308
  60.6 1.3 %copy-start.1 = (f32[7,128,128]{2,1,0:T(8,128)S(1)}, f32[7,128,128]{2,1,0:T(8,128)}, u32[]{:S(2)}) copy-start(f32[7,128,128]{2,1,0:T(8,128)} %get-tuple-element.25) | copy-start | bytes 1376260
  61.9 0.8 %copy-start.3 = (f32[64,128]{1,0:T(8,128)S(1)}, f32[64,128]{1,0:T(8,128)}, u32[]{:S(2)}) copy-start(f32[64,128]{1,0:T(8,128)} %get-tuple-element.27) | copy-start | bytes 98308

commit v2 on v1

--- a/solution.py
+++ b/solution.py
@@ -16,8 +16,8 @@
 ROWS = 512
 LANES = 512
 SLOT_ROWS = 16
-PART_ROWS = 1280
-UNITS = 10
+COARSE_ROWS = 1024
+FINE_ROWS = 256
 
 
 def iota(shape, axis):
@@ -34,6 +34,10 @@
 
 def dot_tn(a, b):
     return lax.dot_general(a, b, (((0,), (0,)), ((), ())), preferred_element_type=F32)
+
+
+def exact_dot(a, b):
+    return jnp.dot(a, b, precision=lax.Precision.HIGHEST, preferred_element_type=F32)
 
 
 def one_hot(condition):
@@ -124,11 +128,9 @@
     frequency_ref,
     mixed_ref,
     input_grad_ref,
-    fine_grad_ref,
-    down_grad_ref,
-    coarse_grad_ref,
-    up_grad_ref,
-    time_grad_ref,
+    coarse_sum_ref,
+    fine_sum_ref,
+    time_sum_ref,
     small_out,
     small_in,
     face_out,
@@ -137,17 +139,20 @@
     rim_in,
     back_out,
     back_in,
-    part_out,
-    part_in,
-    unit_out,
-    unit_in,
-    sum_out,
-    sum_in,
-    whole,
-    time_out,
-    time_in,
-    time_mid,
-    time_whole,
+    pair_out,
+    pair_in,
+    coarse_out_ref,
+    coarse_in,
+    coarse_mid,
+    coarse_all,
+    fine_out,
+    fine_in,
+    fine_mid,
+    fine_all,
+    brick_all,
+    time_all,
+    mixed_held,
+    input_grad_held,
     hot_halo,
     hot_out,
     table,
@@ -159,13 +164,13 @@
     band_ref,
     send_sems,
     recv_sems,
+    copy_sems,
 ):
     grp = lax.axis_index("grp")
     dev = lax.axis_index("dev")
-    units = UNITS
-    unit_rows = PART_ROWS // n_grp // units
-    owners = min(n_grp, 8)
-    owner_rows = 64 // owners
+    chip = dev // 2
+    core = dev % 2
+    n_chip = n_dev // 2
 
     def entry_signal():
         barrier = pltpu.get_barrier_semaphore()
@@ -202,30 +207,37 @@
             device_id_type=pl.DeviceIdType.MESH,
         )
 
-    def position(along):
-        return (dev, n_dev) if along == "dev" else (grp, n_grp)
+    def ring(along):
+        if along == "dev":
+            return dev, n_dev, "dev", lambda p: p
+        if along == "chip":
+            return chip, n_chip, "dev", lambda p: 2 * p + core
+        if along == "core":
+            return core, 2, "dev", lambda p: 2 * chip + p
+        return grp, n_grp, "grp", lambda p: p
 
     def exchange(src, dst, index, along):
-        me, count = position(along)
+        me, count, axis, device = ring(along)
 
         def step(j, carry):
             p = lax.rem(me + j, count)
-            remote(src.at[p], dst.at[me], index, along, p).start()
+            remote(src(p), dst, index, axis, device(p)).start()
             return carry
 
         lax.fori_loop(1, count, step, 0)
 
-    def wait_arrived(dst, blocks, index, along):
-        me, count = position(along)
-        if blocks > 0:
-            part = dst.at[pl.ds(0, blocks)]
-            remote(part, part, index, along, lax.rem(me + 1, count)).wait_recv()
-
-    def wait_sent(src, blocks, index, along):
-        me, count = position(along)
-        if blocks > 0:
-            part = src.at[pl.ds(0, blocks)]
-            remote(part, part, index, along, lax.rem(me + 1, count)).wait_send()
+    def wait_arrived(part, index, along):
+        me, count, axis, device = ring(along)
+        if count > 1:
+            remote(part, part, index, axis, device(lax.rem(me + 1, count))).wait_recv()
+
+    def wait_sent(part, index, along):
+        me, count, axis, device = ring(along)
+        if count > 1:
+            remote(part, part, index, axis, device(lax.rem(me + 1, count))).wait_send()
+
+    def others(ref, count):
+        return ref.at[pl.ds(0, max(count - 1, 1))]
 
     entry_signal()
 
@@ -237,9 +249,11 @@
         return iota(shape, 0), iota(shape, 1)
 
     i, j = spread_index((n_dev, n_dev * SLOT_ROWS))
-    sources = sources_ref[0].astype(F32)
-    chosen = jnp.where(((j >> 3) & 1) == 0, sources[:, 0:1], sources[:, 1:2])
-    code = jnp.sum(jnp.where((j >> 4) == i, chosen, 0.0), axis=0, keepdims=True)
+    by_slot = (j >> 4) == i
+    spread_slot = jnp.where(by_slot, 1.0, 0.0)
+    sources = exact_dot(sources_ref[0].astype(F32), spread_slot)
+    j = iota((1, n_dev * SLOT_ROWS), 1)
+    code = jnp.where(((j >> 3) & 1) == 0, sources[0:1], sources[1:2])
     brick = jnp.zeros_like(code)
     for m in range(1, BRICKS):
         brick = brick + jnp.where(code > 6.0 * m - 0.5, 1.0, 0.0)
@@ -304,12 +318,7 @@
     step_column = jnp.sum(jnp.where(i == j, steps, 0.0), axis=1, keepdims=True)
     angles = step_column * frequency_ref[...]
     embedding = jnp.where(iota((BRICKS, 64), 1) < 32, jnp.cos(angles), jnp.sin(angles))
-    modulate = jnp.dot(
-        embedding,
-        time_weight_ref[...],
-        precision=lax.Precision.HIGHEST,
-        preferred_element_type=F32,
-    )
+    modulate = exact_dot(embedding, time_weight_ref[...])
     swapped = pltpu.roll(modulate, 64, 1)
     low_b = iota((BRICKS, 128), 1) < 64
     scale = lanes_four(jnp.where(low_b, modulate, swapped))
@@ -328,11 +337,17 @@
     pooled = fold_lanes(jnp.where(half_mask, dot(pool, active), 0.0)) * (1.0 / 64.0)
     grad_up = fold_lanes(jnp.where(half_mask, dot(pool, grad_b), 0.0))
     small = jnp.where(low_half, pooled, grad_up).astype(BF16)
-    small_out[...] = dot_tn(hot_target, small).astype(BF16).reshape(n_dev, SLOT_ROWS, 128)
+    i, j = spread_index((BRICKS, 128))
+    wide_embedding = jnp.concatenate([embedding, embedding], axis=1)
+    rounded = wide_embedding.astype(BF16).astype(F32)
+    rounded = jnp.where(j < 64, rounded, wide_embedding - rounded)
+    rounded = jnp.concatenate([jnp.zeros((8, 128), F32), rounded] * n_dev, axis=0)
+    small = dot_tn(hot_target, small) + rounded
+    small_out[...] = small.astype(BF16).reshape(n_dev, SLOT_ROWS, 128)
     small_in[dev] = small_out[dev]
     barrier = pltpu.get_barrier_semaphore()
     pl.semaphore_wait(barrier, n_dev - 1 + n_grp - 1)
-    exchange(small_out, small_in, 0, "dev")
+    exchange(lambda p: small_out.at[p], small_in.at[dev], 0, "dev")
 
     z_first, z_last = z_table(active, y_mask, select_x)
     table[512:576, :] = z_first
@@ -341,7 +356,7 @@
         dot_tn(hot_out[...], table[...]).astype(BF16).reshape(n_dev, SLOT_ROWS, LANES)
     )
     face_in[dev] = face_out[dev]
-    exchange(face_out, face_in, 1, "dev")
+    exchange(lambda p: face_out.at[p], face_in.at[dev], 1, "dev")
 
     i, j = spread_index((64, LANES))
     wide = dot(fine_weight_ref[...].reshape(448, 64), one_hot(i == (j & 63)))
@@ -392,7 +407,7 @@
         .reshape(n_dev, SLOT_ROWS, LANES)
     )
     rim_in[dev] = rim_out[dev]
-    exchange(rim_out, rim_in, 2, "dev")
+    exchange(lambda p: rim_out.at[p], rim_in.at[dev], 2, "dev")
 
     x_at, y_at = (row >> 3) & 7, row & 7
 
@@ -417,10 +432,8 @@
     grad_t = grad.T.astype(BF16)
     center = dot(grad_t, active)
 
-    wait_arrived(small_in, n_dev - 1, 0, "dev")
-    i, j = spread_index((n_dev, n_dev * SLOT_ROWS))
-    places = places_ref[0].astype(F32)
-    place = jnp.sum(jnp.where((j >> 4) == i, places, 0.0), axis=0, keepdims=True)
+    wait_arrived(others(small_in, n_dev), 0, "dev")
+    place = exact_dot(places_ref[...].astype(F32), spread_slot)
     j = iota((1, n_dev * SLOT_ROWS), 1)
     place_code = (place * 8 + (j & 7).astype(F32)).astype(jnp.int32)
     i = iota((ROWS, 1), 0)
@@ -435,8 +448,7 @@
     hot_place_grad = one_hot(voxel_code == jnp.where(first_kind, -1, place_code))
     grid = dot(hot_place, small_in[...].reshape(n_dev * SLOT_ROWS, 128)).astype(BF16)
     down = jnp.concatenate([down_weight_ref[...], jnp.zeros((64, 128), BF16)], axis=0)
-    i, j = spread_index((64, 128))
-    up = dot(up_weight_ref[...], one_hot(j - 64 == i)).astype(BF16)
+    up = jnp.concatenate([jnp.zeros((64, 128), BF16), up_weight_ref[...]], axis=0)
     coarse_pre = dot(grid, down)
     coarse_sig = 1.0 / (1.0 + jnp.exp(-coarse_pre))
     coarse_act = coarse_pre * coarse_sig
@@ -454,7 +466,7 @@
         axis=1,
     )
     coarse_out = dot(stack, coarse_weight_ref[...].reshape(896, 128)).astype(BF16)
-    grad_out = dot_nt(grid, up)
+    grad_out = dot(grid, up)
     grad_out_b = grad_out.astype(BF16)
     grad_act = dot_nt(grad_out_b, coarse_weight_ref[0])
     for k in range(6):
@@ -470,94 +482,93 @@
         .reshape(n_dev, SLOT_ROWS, 128)
     )
     back_in[dev] = back_out[dev]
-    exchange(back_out, back_in, 3, "dev")
+    exchange(lambda p: back_out.at[p], back_in.at[dev], 3, "dev")
     coarse_grad = dot_tn(stack, grad_out_b)
     down_grad = dot_tn(grid, grad_pre)
-    up_grad = dot_tn(coarse_out, grid)
-    up_rows = jnp.where(low_half, pltpu.roll(up_grad[0:64], 64, 1), up_grad[64:128])
-
-    wait_arrived(face_in, n_dev - 1, 1, "dev")
+    up_grad = dot_tn(grid, coarse_out)
+
+    part = jnp.concatenate([coarse_grad, down_grad[0:64], up_grad[64:128]], axis=0)
+    pair_out[...] = part.astype(BF16).reshape(2, COARSE_ROWS // 2, 128)
+    exchange(lambda p: pair_out.at[p], pair_in, 4, "core")
+
+    wait_arrived(others(face_in, n_dev), 1, "dev")
     halo = dot_tn(hot_halo[0:640, :], table[...]) + dot_tn(
         hot_halo[640 : 640 + n_dev * SLOT_ROWS, :],
         face_in[...].reshape(n_dev * SLOT_ROWS, LANES),
     )
     halo = halo.astype(BF16)
     tap_grads = [diagonal_sum(center, 0, 0, 8)]
-    conv = conv_ref[...]
-    left, right = conv[:, 0:256], conv[:, 256:512]
+    taps = []
     for k in range(4):
         repeat = repeat_x if k < 2 else repeat_y
         moved = shifted(active_f, k, dot(repeat, halo[64 * k : 64 * k + 64])).astype(BF16)
-        band = band_ref[256 * k : 256 * (k + 1), :]
-        left = left + dot(moved[:, 0:256], band)
-        right = right + dot(moved[:, 256:512], band)
+        taps.append(moved)
         tap_grads.append(
             diagonal_sum(dot(grad_t[0:256], moved[:, 0:256]), 0, 0, 4)
             + diagonal_sum(dot(grad_t[256:512], moved[:, 256:512]), 0, 0, 4)
         )
-    layer = jnp.where(y_mask, dot(repeat_y, halo[256:320]), 0.0).astype(BF16)
-    tail = jnp.concatenate(
-        [jnp.where(low_half, weight_ref[320:384, 0:128], 0.0).astype(BF16)] * 8, axis=0
-    )
-    left = jnp.concatenate([left[:, 0:128] + dot(layer, tail), left[:, 128:256]], axis=1)
-    tap_grads.append(
-        diagonal_sum(center, 0, -1, 8) + fold_lanes(dot(grad_t[0:64], layer))
-    )
-    layer = jnp.where(y_mask, dot(repeat_y, halo[320:384]), 0.0).astype(BF16)
-    tail = jnp.concatenate(
-        [jnp.where(low_half, 0.0, weight_ref[384:448, 0:128]).astype(BF16)] * 8, axis=0
-    )
-    right = jnp.concatenate([right[:, 0:128], right[:, 128:256] + dot(layer, tail)], axis=1)
-    tap_grads.append(
-        diagonal_sum(center, 0, 1, 8) + fold_lanes(dot(grad_t[448:512], layer))
-    )
-    conv_ref[...] = jnp.concatenate([left, right], axis=1)
-
+    low_z = jnp.where(y_mask, dot(repeat_y, halo[256:320]), 0.0).astype(BF16)
+    high_z = jnp.where(y_mask, dot(repeat_y, halo[320:384]), 0.0).astype(BF16)
+    tap_grads.append(diagonal_sum(center, 0, -1, 8) + fold_lanes(dot(grad_t[0:64], low_z)))
+    tap_grads.append(diagonal_sum(center, 0, 1, 8) + fold_lanes(dot(grad_t[448:512], high_z)))
     fine_rows = []
     for t in range(4):
         low = tap_grads[t].T[0:64]
         high = tap_grads[t + 4].T[0:64] if t < 3 else jnp.zeros_like(low)
         fine_rows.append(jnp.concatenate([low, high], axis=1))
-    part = jnp.concatenate([coarse_grad, down_grad[0:64], up_rows] + fine_rows, axis=0)
-    part_out[...] = part.astype(BF16).reshape(n_grp, PART_ROWS // n_grp, 128)
-    part_in[grp] = part_out[grp]
-    exchange(part_out, part_in, 4, "grp")
-
-    wait_arrived(back_in, n_dev - 1, 3, "dev")
+    part = jnp.concatenate(fine_rows, axis=0)
+    fine_out[...] = part.astype(BF16).reshape(n_grp, FINE_ROWS // n_grp, 128)
+    fine_in[grp] = fine_out[grp]
+    exchange(lambda p: fine_out.at[p], fine_in.at[grp], 9, "grp")
+
+    wait_arrived(pair_in, 4, "core")
+    part = pair_out[core].astype(F32) + pair_in[...].astype(F32)
+    coarse_out_ref[...] = part.astype(BF16).reshape(n_grp, COARSE_ROWS // 2 // n_grp, 128)
+    coarse_in[grp] = coarse_out_ref[grp]
+    exchange(lambda p: coarse_out_ref.at[p], coarse_in.at[grp], 5, "grp")
+
+    conv = conv_ref[...]
+    left, right = conv[:, 0:256], conv[:, 256:512]
+    for k in range(4):
+        band = band_ref[256 * k : 256 * (k + 1), :]
+        left = left + dot(taps[k][:, 0:256], band)
+        right = right + dot(taps[k][:, 256:512], band)
+    end = jnp.where(low_half, weight_ref[320:384, 0:128], 0.0).astype(BF16)
+    first = dot(low_z, jnp.concatenate([end] * 8, axis=0))
+    end = jnp.where(low_half, 0.0, weight_ref[384:448, 0:128]).astype(BF16)
+    last = dot(high_z, jnp.concatenate([end] * 8, axis=0))
+    conv_ref[...] = jnp.concatenate(
+        [left[:, 0:128] + first, left[:, 128:256], right[:, 0:128], right[:, 128:256] + last],
+        axis=1,
+    )
+
+    wait_arrived(others(coarse_in, n_grp), 5, "grp")
+    part = coarse_in[0].astype(F32)
+    for p in range(1, n_grp):
+        part = part + coarse_in[p].astype(F32)
+    coarse_mid[chip] = part.astype(BF16)
+    exchange(lambda p: coarse_mid.at[chip], coarse_mid.at[chip], 6, "chip")
+
+    wait_arrived(others(back_in, n_dev), 3, "dev")
     back = back_in[...].reshape(n_dev * SLOT_ROWS, 128)
     coarse_values = dot(hot_target, back).astype(BF16)
     i, j = spread_index((64, LANES))
-    up_wide = dot(up_weight_ref[...], one_hot(i == (j & 63))).astype(BF16)
+    up_wide = dot_tn(up_weight_ref[...], one_hot(i == (j & 63))).astype(BF16)
     upward = jnp.where(half_mask, dot(coarse_values, up_wide), 0.0)
     upward_high = upward.astype(BF16)
     upward_low = (upward - upward_high.astype(F32)).astype(BF16)
     upward = dot(unpool, upward_high) + dot(unpool, upward_low)
     features = features_ref[...].astype(F32).reshape(ROWS, LANES)
     mixed = features + conv_ref[...] + upward
-    mixed_ref[...] = mixed.reshape(BRICKS, 8, 8, LANES).astype(BF16)
-
-    wait_arrived(part_in, n_grp - 1, 4, "grp")
-    own = part_in[0].astype(F32)
-    for p in range(1, n_grp):
-        own = own + part_in[p].astype(F32)
-    unit_out[...] = own.reshape(units, unit_rows, 128)
-
-    def to_owner(j, carry):
-        p = lax.rem(dev + j, n_dev)
-
-        @pl.when(p < units)
-        def _():
-            remote(unit_out.at[p], unit_in.at[dev], 5, "dev", p).start()
-
-        return carry
-
-    lax.fori_loop(1, n_dev, to_owner, 0)
+    mixed_held[...] = mixed.reshape(BRICKS, 8, 8, LANES).astype(BF16)
+    mixed_copy = pltpu.make_async_copy(mixed_held, mixed_ref, copy_sems.at[0])
+    mixed_copy.start()
 
     back_grad = dot(hot_target_grad, back).astype(BF16)
     i, j = spread_index((128, LANES))
     back_wide = jnp.where(half_mask, dot(back_grad, one_hot(i == (j & 63))), 0.0)
     total = grad_ref[...] + dot(unpool, (back_wide * (1.0 / 64.0)).astype(BF16))
-    wait_arrived(rim_in, n_dev - 1, 2, "dev")
+    wait_arrived(others(rim_in, n_dev), 2, "dev")
     rim_back = rim_in[...].reshape(n_dev * SLOT_ROWS, LANES)
     total = total + dot(hot_out[0:512, :], rim_back)
     z_rows = (z_rows + dot(hot_out[512:640, :], rim_back)).astype(BF16)
@@ -574,175 +585,141 @@
     )
     normed = normed_ref[...]
     grad_before = total * slope_ref[...]
+    grad_ref[...] = grad_before
     grad_scale = fold_lanes(brick_sum(grad_before * normed))
     grad_shift = fold_lanes(brick_sum(grad_before))
-    time_grad = lax.dot_general(
-        embedding,
-        jnp.where(low_b, grad_scale, grad_shift),
-        (((0,), (0,)), ((), ())),
-        precision=lax.Precision.HIGHEST,
-        preferred_element_type=F32,
-    )
-    time_out[...] = time_grad.reshape(owners, owner_rows, 128)
-
-    def to_time_owner(j, carry):
-        p = lax.rem(grp + j, n_grp)
-
-        @pl.when(p < owners)
-        def _():
-            remote(time_out.at[p], time_in.at[grp], 8, "grp", p).start()
-
-        return carry
-
-    lax.fori_loop(1, n_grp, to_time_owner, 0)
-
-    @pl.when(dev < units)
-    def _():
-        unit_in[dev] = unit_out[dev]
-        wait_arrived(unit_in, n_dev - 1, 5, "dev")
-        mine = unit_in[0]
-        for p in range(1, n_dev):
-            mine = mine + unit_in[p]
-        sum_out[...] = mine
-        sum_in[dev] = mine
-
-        def to_all(j, carry):
-            p = lax.rem(dev + j, n_dev)
-            remote(sum_out, sum_in.at[dev], 6, "dev", p).start()
-            return carry
-
-        lax.fori_loop(1, n_dev, to_all, 0)
-
+    brick_all[dev] = jnp.where(low_b, grad_scale, grad_shift)
+    exchange(lambda p: brick_all.at[dev], brick_all.at[dev], 11, "dev")
+
+    wait_arrived(others(fine_in, n_grp), 9, "grp")
+    part = fine_in[0].astype(F32)
+    for p in range(1, n_grp):
+        part = part + fine_in[p].astype(F32)
+    fine_mid[dev] = part.astype(BF16)
+    exchange(lambda p: fine_mid.at[dev], fine_mid.at[dev], 10, "dev")
+
+    wait_arrived(others(coarse_mid, n_chip), 6, "chip")
+    part = coarse_mid[0].astype(F32)
+    for p in range(1, n_chip):
+        part = part + coarse_mid[p].astype(F32)
+    coarse_all[core, grp] = part.astype(BF16)
+    exchange(lambda p: coarse_all.at[core, grp], coarse_all.at[core, grp], 7, "grp")
+
+    grad_before = grad_ref[...]
     g3 = grad_before.reshape(BRICKS, 64, LANES) * per_brick(gain)
-    n3 = normed.reshape(BRICKS, 64, LANES)
+    n3 = normed_ref[...].reshape(BRICKS, 64, LANES)
     mean_g = group_mean(jnp.sum(g3, axis=1))
     mean_gn = group_mean(jnp.sum(g3 * n3, axis=1))
     result = per_brick(inverse) * (g3 - per_brick(mean_g) - n3 * per_brick(mean_gn))
     grad = cotangent_ref[...].astype(F32).reshape(ROWS, LANES)
     result = grad + result.reshape(ROWS, LANES)
-    input_grad_ref[...] = result.reshape(BRICKS, 8, 8, LANES).astype(BF16)
-
-    @pl.when(grp < owners)
-    def _():
-        time_in[grp] = time_out[grp]
-        wait_arrived(time_in, n_grp - 1, 8, "grp")
-        mine = time_in[0]
-        for p in range(1, n_grp):
-            mine = mine + time_in[p]
-        time_mid[dev] = mine
-
-        def to_all(j, carry):
-            p = lax.rem(dev + j, n_dev)
-            remote(time_mid.at[dev], time_mid.at[dev], 9, "dev", p).start()
-            return carry
-
-        lax.fori_loop(1, n_dev, to_all, 0)
-
-    @pl.when(dev < units)
-    def _():
-        wait_arrived(sum_in, units - 1, 6, "dev")
-
-    @pl.when(dev >= units)
-    def _():
-        wait_arrived(sum_in, units, 6, "dev")
-
-    whole[grp] = sum_in[...].reshape(units * unit_rows, 128).astype(BF16)
-
-    def to_all(j, carry):
-        p = lax.rem(grp + j, n_grp)
-        remote(whole.at[grp], whole.at[grp], 7, "grp", p).start()
-        return carry
-
-    lax.fori_loop(1, n_grp, to_all, 0)
-
-    @pl.when(grp < owners)
-    def _():
-        wait_arrived(time_mid, n_dev - 1, 9, "dev")
-        mine = time_mid[0]
-        for p in range(1, n_dev):
-            mine = mine + time_mid[p]
-        time_whole[grp] = mine
-
-        def to_all(j, carry):
-            p = lax.rem(grp + j, n_grp)
-            remote(time_whole.at[grp], time_whole.at[grp], 10, "grp", p).start()
-            return carry
-
-        lax.fori_loop(1, n_grp, to_all, 0)
-
-    wait_arrived(whole, n_grp - 1, 7, "grp")
-    sums = whole[...].reshape(PART_ROWS, 128).astype(F32)
-    coarse_grad_ref[...] = sums[0:896].reshape(7, 128, 128)
-    down_grad_ref[...] = sums[896:960]
-    up_grad_ref[0:64, :] = sums[960:1024, 0:64]
-    up_grad_ref[64:128, :] = pltpu.roll(sums[960:1024], 64, 1)[:, 0:64]
+    input_grad_held[...] = result.reshape(BRICKS, 8, 8, LANES).astype(BF16)
+    input_grad_copy = pltpu.make_async_copy(input_grad_held, input_grad_ref, copy_sems.at[1])
+    input_grad_copy.start()
+
+    wait_arrived(others(fine_mid, n_dev), 10, "dev")
+    part = fine_mid[0].astype(F32)
+    for p in range(1, n_dev):
+        part = part + fine_mid[p].astype(F32)
+    fine_all[grp] = part.astype(BF16)
+    exchange(lambda p: fine_all.at[grp], fine_all.at[grp], 12, "grp")
+
+    wait_arrived(others(brick_all, n_dev), 11, "dev")
+    embeddings = small_in[...].astype(F32)[:, 8:16, :].reshape(n_dev * BRICKS, 128)
+    embeddings = embeddings + pltpu.roll(embeddings, 64, 1)
+    time_grad = lax.dot_general(
+        embeddings,
+        brick_all[...].reshape(n_dev * BRICKS, 128),
+        (((0,), (0,)), ((), ())),
+        precision=lax.Precision.HIGHEST,
+        preferred_element_type=F32,
+    )
+    time_all[grp] = time_grad[0:64].astype(BF16)
+    exchange(lambda p: time_all.at[grp], time_all.at[grp], 13, "grp")
+
+    wait_arrived(others(coarse_all.at[0], n_grp), 7, "grp")
+    exchange(lambda p: coarse_all.at[core], coarse_all.at[core], 8, "core")
+    wait_arrived(others(fine_all, n_grp), 12, "grp")
+    fine_sum_ref[...] = fine_all[...].reshape(FINE_ROWS, 128)
+    wait_arrived(coarse_all.at[0], 8, "core")
+    coarse_sum_ref[...] = coarse_all[...].reshape(COARSE_ROWS, 128)
+    wait_arrived(others(time_all, n_grp), 13, "grp")
+    part = time_all[0].astype(F32)
+    for p in range(1, n_grp):
+        part = part + time_all[p].astype(F32)
+    time_sum_ref[...] = part
+
+    wait_sent(others(small_out, n_dev), 0, "dev")
+    wait_sent(others(face_out, n_dev), 1, "dev")
+    wait_sent(others(rim_out, n_dev), 2, "dev")
+    wait_sent(others(back_out, n_dev), 3, "dev")
+    wait_sent(pair_in, 4, "core")
+    wait_sent(others(coarse_out_ref, n_grp), 5, "grp")
+    wait_sent(others(coarse_mid, n_chip), 6, "chip")
+    wait_sent(others(coarse_all.at[0], n_grp), 7, "grp")
+    wait_sent(coarse_all.at[0], 8, "core")
+    wait_sent(others(fine_out, n_grp), 9, "grp")
+    wait_sent(others(fine_mid, n_dev), 10, "dev")
+    wait_sent(others(brick_all, n_dev), 11, "dev")
+    wait_sent(others(fine_all, n_grp), 12, "grp")
+    wait_sent(others(time_all, n_grp), 13, "grp")
+    mixed_copy.wait()
+    input_grad_copy.wait()
+
+
+def finish(
+    mixed_in,
+    input_grad_in,
+    coarse_sum_ref,
+    fine_sum_ref,
+    time_sum_ref,
+    mixed_ref,
+    input_grad_ref,
+    fine_grad_ref,
+    down_grad_ref,
+    coarse_grad_ref,
+    up_grad_ref,
+    time_grad_ref,
+):
+    mixed_ref[...] = mixed_in[...]
+    input_grad_ref[...] = input_grad_in[...]
+    coarse_grad_ref[...] = coarse_sum_ref[0:896, :].astype(F32).reshape(7, 128, 128)
+    down_grad_ref[...] = coarse_sum_ref[896:960, :].astype(F32)
+    up_grad_ref[...] = coarse_sum_ref[960:1024, :].astype(F32)
     for t in range(4):
-        piece = sums[1024 + 64 * t : 1088 + 64 * t]
+        piece = fine_sum_ref[64 * t : 64 * t + 64, :].astype(F32)
         fine_grad_ref[t] = piece[:, 0:64]
         if t < 3:
             fine_grad_ref[t + 4] = pltpu.roll(piece, 64, 1)[:, 0:64]
-
-    @pl.when(grp < owners)
-    def _():
-        wait_arrived(time_whole, owners - 1, 10, "grp")
-
-    @pl.when(grp >= owners)
-    def _():
-        wait_arrived(time_whole, owners, 10, "grp")
-
-    time_grad_ref[...] = time_whole[...].reshape(64, 128)
-
-    wait_sent(small_out, n_dev - 1, 0, "dev")
-    wait_sent(face_out, n_dev - 1, 1, "dev")
-    wait_sent(rim_out, n_dev - 1, 2, "dev")
-    wait_sent(back_out, n_dev - 1, 3, "dev")
-    wait_sent(part_out, n_grp - 1, 4, "grp")
-    wait_sent(whole, n_grp - 1, 7, "grp")
-
-    @pl.when(dev < units)
-    def _():
-        wait_sent(unit_out, units - 1, 5, "dev")
-        wait_sent(unit_in, n_dev - 1, 6, "dev")
-
-    @pl.when(dev >= units)
-    def _():
-        wait_sent(unit_out, units, 5, "dev")
-
-    @pl.when(grp < owners)
-    def _():
-        wait_sent(time_out, owners - 1, 8, "grp")
-        wait_sent(time_mid, n_dev - 1, 9, "dev")
-        wait_sent(time_in, n_grp - 1, 10, "grp")
-
-    @pl.when(grp >= owners)
-    def _():
-        wait_sent(time_out, owners, 8, "grp")
+    time_grad_ref[...] = time_sum_ref[...]
 
 
 def body(n_grp, n_dev, *args):
     half = 32
     frequency = np.exp(-math.log(10000.0) * np.arange(half) / half).astype(np.float32)
     frequency = jnp.asarray(np.concatenate([frequency, frequency])[None, :])
-    chunk = PART_ROWS // n_grp
-    units, unit_rows = UNITS, chunk // UNITS
-    owners = min(n_grp, 8)
-    owner_rows = 64 // owners
+    args = list(args)
+    args[4] = jnp.swapaxes(args[4], 1, 2)
+    args[6] = args[6].reshape(1, n_dev)
+    args[11] = args[11].T
     vmem = pl.BlockSpec(memory_space=pltpu.VMEM)
+    free = pl.BlockSpec(memory_space=pl.ANY)
     packed = jax.ShapeDtypeStruct((BRICKS, 8, 8, LANES), BF16)
     slots = (n_dev, SLOT_ROWS)
-    return pl.pallas_call(
+    coarse_half = COARSE_ROWS // 2
+    coarse_chunk = coarse_half // n_grp
+    fine_chunk = FINE_ROWS // n_grp
+    held = pl.pallas_call(
         functools.partial(kernel, n_grp, n_dev),
         out_shape=(
             packed,
             packed,
-            jax.ShapeDtypeStruct((7, 64, 64), F32),
-            jax.ShapeDtypeStruct((64, 128), F32),
-            jax.ShapeDtypeStruct((7, 128, 128), F32),
-            jax.ShapeDtypeStruct((128, 64), F32),
+            jax.ShapeDtypeStruct((COARSE_ROWS, 128), BF16),
+            jax.ShapeDtypeStruct((FINE_ROWS, 128), BF16),
             jax.ShapeDtypeStruct((64, 128), F32),
         ),
         in_specs=[vmem] * 13,
-        out_specs=(vmem,) * 7,
+        out_specs=(free, free, vmem, vmem, vmem),
         scratch_shapes=[
             pltpu.VMEM(slots + (128,), BF16),
             pltpu.VMEM(slots + (128,), BF16),
@@ -752,17 +729,20 @@
             pltpu.VMEM(slots + (LANES,), BF16),
             pltpu.VMEM(slots + (128,), BF16),
             pltpu.VMEM(slots + (128,), BF16),
-            pltpu.VMEM((n_grp, chunk, 128), BF16),
-            pltpu.VMEM((n_grp, chunk, 128), BF16),
-            pltpu.VMEM((units, unit_rows, 128), F32),
-            pltpu.VMEM((n_dev, unit_rows, 128), F32),
-            pltpu.VMEM((unit_rows, 128), F32),
-            pltpu.VMEM((units, unit_rows, 128), F32),
-            pltpu.VMEM((n_grp, chunk, 128), BF16),
-            pltpu.VMEM((owners, owner_rows, 128), F32),
-            pltpu.VMEM((n_grp, owner_rows, 128), F32),
-            pltpu.VMEM((n_dev, owner_rows, 128), F32),
-            pltpu.VMEM((owners, owner_rows, 128), F32),
+            pltpu.VMEM((2, coarse_half, 128), BF16),
+            pltpu.VMEM((coarse_half, 128), BF16),
+            pltpu.VMEM((n_grp, coarse_chunk, 128), BF16),
+            pltpu.VMEM((n_grp, coarse_chunk, 128), BF16),
+            pltpu.VMEM((n_dev // 2, coarse_chunk, 128), BF16),
+            pltpu.VMEM((2, n_grp, coarse_chunk, 128), BF16),
+            pltpu.VMEM((n_grp, fine_chunk, 128), BF16),
+            pltpu.VMEM((n_grp, fine_chunk, 128), BF16),
+            pltpu.VMEM((n_dev, fine_chunk, 128), BF16),
+            pltpu.VMEM((n_grp, fine_chunk, 128), BF16),
+            pltpu.VMEM((n_dev, BRICKS, 128), F32),
+            pltpu.VMEM((n_grp, 64, 128), BF16),
+            pltpu.VMEM((BRICKS, 8, 8, LANES), BF16),
+            pltpu.VMEM((BRICKS, 8, 8, LANES), BF16),
             pltpu.VMEM((640 + n_dev * SLOT_ROWS, 384), BF16),
             pltpu.VMEM((640, n_dev * SLOT_ROWS), BF16),
             pltpu.VMEM((640, LANES), BF16),
@@ -772,13 +752,30 @@
             pltpu.VMEM((ROWS, LANES), F32),
             pltpu.VMEM((448, LANES), F32),
             pltpu.VMEM((1536, 256), BF16),
-            pltpu.SemaphoreType.DMA((11,)),
-            pltpu.SemaphoreType.DMA((11,)),
+            pltpu.SemaphoreType.DMA((14,)),
+            pltpu.SemaphoreType.DMA((14,)),
+            pltpu.SemaphoreType.DMA((2,)),
         ],
         compiler_params=pltpu.CompilerParams(
             collective_id=0, has_side_effects=True, vmem_limit_bytes=56 * 1024 * 1024
         ),
     )(*args, frequency)
+    outs = pl.pallas_call(
+        finish,
+        out_shape=(
+            packed,
+            packed,
+            jax.ShapeDtypeStruct((7, 64, 64), F32),
+            jax.ShapeDtypeStruct((64, 128), F32),
+            jax.ShapeDtypeStruct((7, 128, 128), F32),
+            jax.ShapeDtypeStruct((64, 128), F32),
+            jax.ShapeDtypeStruct((64, 128), F32),
+        ),
+        in_specs=[vmem] * 5,
+        out_specs=(vmem,) * 7,
+        compiler_params=pltpu.CompilerParams(vmem_limit_bytes=56 * 1024 * 1024),
+    )(*held)
+    return outs[0], outs[1], outs[2], outs[3], outs[4], outs[5].T, outs[6]
 
 
 def solution(mesh):

time: 63.6 us -> 50.7 us (0.80)
  local copies, waits for them, and re-layouts: 10.7 us -> 0 us
  Pallas kernels: 52 us -> 49.9 us
    unnamed x21 -> x0, local copies, waits for them, and re-layouts: 9.16 us -> none
    pallas_call x1, Pallas kernels: 52 us -> 47.4 us  [body(): pl.pallas_call(functools.partial(kernel, n_grp, n_dev), out_shape=(packed...]
    pallas_call x0 -> x1, Pallas kernels: none -> 2.54 us  [body(): pl.pallas_call(finish, out_shape=(packed, packed, jax.ShapeDtypeStruct((7...]
    pallas_call x1 -> x0, local copies, waits for them, and re-layouts: 1.54 us -> none  [body(): pl.pallas_call(functools.partial(kernel, n_grp, n_dev), out_shape=(packed...]
where the time goes in v2:
time: 50.7 us; the launch traced here: 50.6 us
  Pallas kernels  49.9 us (98%)
  between operations  0.65 us (1%)
    pallas_call x1, Pallas kernels, body(): pl.pallas_call(functools.partial(kernel, n_grp, n_dev), out_shape=(packed...  47.4 us
    pallas_call x1, Pallas kernels, body(): pl.pallas_call(finish, out_shape=(packed, packed, jax.ShapeDtypeStruct((7...  2.54 us

profile of v2, /device:TPU:1, one launch (start us, length us, event | category | flops | bytes accessed | tf_op | source)
XLA Modules:
  0.0 50.6 jit_solution(14548900653887644600)
XLA Ops:
  0.6 47.4 %shard_map.180 = (bf16[8,8,8,512]{3,2,1,0:T(8,128)(2,1)}, bf16[8,8,8,512]{3,2,1,0:T(8,128)(2,1)}, bf16[1024,128]{1,0:T(8,128)(2,1)}, bf16[256,128]{1,0:T(8,128)(2,1)}, f32[64,128]{1,0:T(8,128)}) custom-call(bf16[8,8,8,512]{3,2,1,0:T(8,128)(2,1)} %features_ref.1, bf16[8,8,8,512]{3,2,1,0:T(8,128)(2,1)} %cotangent_ref.1, s32[8]{0:T(128)} %steps_ref.1, ...), custom_call_target="tpu_custom_call" | custom-call | tf_op jit(solution)/shard_map/pallas_call | solution.py:712
  48.0 2.5 %shard_map.181 = (bf16[8,8,8,512]{3,2,1,0:T(8,128)(2,1)}, bf16[8,8,8,512]{3,2,1,0:T(8,128)(2,1)}, f32[7,64,64]{2,1,0:T(8,128)}, f32[64,128]{1,0:T(8,128)}, f32[7...) custom-call(bf16[8,8,8,512]{3,2,1,0:T(8,128)(2,1)} %get-tuple-element.19.mixed_in, ...), custom_call_target="tpu_custom_call" | custom-call | tf_op jit(solution)/shard_map/pallas_call | solution.py:763

commit v3 on v2

--- a/solution.py
+++ b/solution.py
@@ -113,19 +113,19 @@
 def kernel(
     n_grp,
     n_dev,
-    features_ref,
-    cotangent_ref,
-    steps_ref,
-    links_ref,
-    sources_ref,
-    targets_ref,
-    places_ref,
-    time_weight_ref,
-    fine_weight_ref,
-    down_weight_ref,
-    coarse_weight_ref,
-    up_weight_ref,
-    frequency_ref,
+    features_far,
+    cotangent_far,
+    steps_far,
+    links_far,
+    sources_far,
+    targets_far,
+    places_far,
+    time_weight_far,
+    fine_weight_far,
+    down_weight_far,
+    coarse_weight_far,
+    up_weight_far,
+    frequency_far,
     mixed_ref,
     input_grad_ref,
     coarse_sum_ref,
@@ -135,13 +135,11 @@
     small_in,
     face_out,
     face_in,
-    rim_out,
-    rim_in,
+    layer_out,
+    layer_in,
     back_out,
     back_in,
-    pair_out,
-    pair_in,
-    coarse_out_ref,
+    coarse_part,
     coarse_in,
     coarse_mid,
     coarse_all,
@@ -165,81 +163,117 @@
     send_sems,
     recv_sems,
     copy_sems,
+    features_ref,
+    cotangent_ref,
+    steps_ref,
+    links_ref,
+    sources_ref,
+    targets_ref,
+    places_ref,
+    time_weight_ref,
+    fine_weight_ref,
+    down_weight_ref,
+    coarse_weight_ref,
+    up_weight_ref,
+    frequency_ref,
+    load_sems,
 ):
     grp = lax.axis_index("grp")
     dev = lax.axis_index("dev")
     chip = dev // 2
     core = dev % 2
     n_chip = n_dev // 2
+    coarse_chunk = COARSE_ROWS // 2 // n_grp
+
+    rings = {
+        "dev": (dev, n_dev, lambda p: (grp, p)),
+        "chip": (chip, n_chip, lambda p: (grp, 2 * p + core)),
+        "grp": (grp, n_grp, lambda p: (p, dev)),
+        "cross": (grp, n_grp, lambda p: (p, 2 * chip + 1 - core)),
+        "plane": (2 * grp + core, 2 * n_grp, lambda p: (p // 2, 2 * chip + p % 2)),
+    }
+
+    def device_at(along, p):
+        grp_at, dev_at = rings[along][2](p)
+        return {"grp": grp_at, "dev": dev_at}
 
     def entry_signal():
         barrier = pltpu.get_barrier_semaphore()
-
-        def to_dev(j, carry):
-            pl.semaphore_signal(
-                barrier,
-                inc=1,
-                device_id={"grp": grp, "dev": lax.rem(dev + j, n_dev)},
-                device_id_type=pl.DeviceIdType.MESH,
-            )
-            return carry
-
-        def to_grp(j, carry):
-            pl.semaphore_signal(
-                barrier,
-                inc=1,
-                device_id={"grp": lax.rem(grp + j, n_grp), "dev": dev},
-                device_id_type=pl.DeviceIdType.MESH,
-            )
-            return carry
-
-        lax.fori_loop(1, n_dev, to_dev, 0)
-        lax.fori_loop(1, n_grp, to_grp, 0)
-
-    def remote(src, dst, index, along, peer):
-        target = {"grp": grp, "dev": peer} if along == "dev" else {"grp": peer, "dev": dev}
+        for along in ("dev", "grp", "cross"):
+            me, count, _ = rings[along]
+
+            def step(j, carry, along=along, me=me, count=count):
+                pl.semaphore_signal(
+                    barrier,
+                    inc=1,
+                    device_id=device_at(along, lax.rem(me + j, count)),
+                    device_id_type=pl.DeviceIdType.MESH,
+                )
+                return carry
+
+            lax.fori_loop(1, count, step, 0)
+
+    def entry_wait():
+        pl.semaphore_wait(pltpu.get_barrier_semaphore(), n_dev - 1 + 2 * (n_grp - 1))
+
+    def remote(src, dst, index, along, p):
         return pltpu.make_async_remote_copy(
             src_ref=src,
             dst_ref=dst,
             send_sem=send_sems.at[index],
             recv_sem=recv_sems.at[index],
-            device_id=target,
+            device_id=device_at(along, p),
             device_id_type=pl.DeviceIdType.MESH,
         )
 
-    def ring(along):
-        if along == "dev":
-            return dev, n_dev, "dev", lambda p: p
-        if along == "chip":
-            return chip, n_chip, "dev", lambda p: 2 * p + core
-        if along == "core":
-            return core, 2, "dev", lambda p: 2 * chip + p
-        return grp, n_grp, "grp", lambda p: p
-
     def exchange(src, dst, index, along):
-        me, count, axis, device = ring(along)
+        me, count, _ = rings[along]
 
         def step(j, carry):
             p = lax.rem(me + j, count)
-            remote(src(p), dst, index, axis, device(p)).start()
+            remote(src(p), dst, index, along, p).start()
             return carry
 
         lax.fori_loop(1, count, step, 0)
 
     def wait_arrived(part, index, along):
-        me, count, axis, device = ring(along)
+        me, count, _ = rings[along]
         if count > 1:
-            remote(part, part, index, axis, device(lax.rem(me + 1, count))).wait_recv()
+            remote(part, part, index, along, lax.rem(me + 1, count)).wait_recv()
 
     def wait_sent(part, index, along):
-        me, count, axis, device = ring(along)
+        me, count, _ = rings[along]
         if count > 1:
-            remote(part, part, index, axis, device(lax.rem(me + 1, count))).wait_send()
+            remote(part, part, index, along, lax.rem(me + 1, count)).wait_send()
 
     def others(ref, count):
         return ref.at[pl.ds(0, max(count - 1, 1))]
 
+    loads = [
+        pltpu.make_async_copy(far, near, load_sems.at[index])
+        for index, (far, near) in enumerate(
+            (
+                (features_far, features_ref),
+                (cotangent_far, cotangent_ref),
+                (steps_far, steps_ref),
+                (links_far, links_ref),
+                (sources_far, sources_ref),
+                (targets_far, targets_ref),
+                (places_far, places_ref),
+                (time_weight_far, time_weight_ref),
+                (fine_weight_far, fine_weight_ref),
+                (down_weight_far, down_weight_ref),
+                (coarse_weight_far, coarse_weight_ref),
+                (up_weight_far, up_weight_ref),
+                (frequency_far, frequency_ref),
+            )
+        )
+    ]
+    for load in loads:
+        load.start()
     entry_signal()
+    for load in loads:
+        load.wait()
 
     row = iota((ROWS, LANES), 0)
     lane = iota((ROWS, LANES), 1)
@@ -305,6 +339,28 @@
     repeat_y = one_hot(j == (i >> 3))
     repeat_x = one_hot(j == ((i >> 6) * 8 + (i & 7)))
     low_half = iota((64, 128), 1) < 64
+
+    grad = cotangent_ref[...].astype(F32).reshape(ROWS, LANES)
+    grad_b = grad.astype(BF16)
+    i, j = spread_index((64, ROWS))
+    g4 = grad.reshape(BRICKS, 8, 8, LANES)
+    grad_z = z_table(grad_b, y_mask, select_x)
+    layers = [
+        g4[:, 0].reshape(64, LANES).astype(BF16),
+        g4[:, 7].reshape(64, LANES).astype(BF16),
+        dot(one_hot(j == i * 8), grad_b).astype(BF16),
+        dot(one_hot(j == i * 8 + 7), grad_b).astype(BF16),
+        grad_z[0],
+        grad_z[1],
+    ]
+    hot_slots = hot_halo[640 : 640 + n_dev * SLOT_ROWS, :]
+    layer_out[...] = (
+        dot(hot_slots, jnp.concatenate(layers, axis=0))
+        .astype(BF16)
+        .reshape(n_dev, SLOT_ROWS, LANES)
+    )
+    layer_in[dev] = layer_out[dev]
+    directions = dot(hot_slots, (iota((384, 128), 0) >> 6).astype(F32).astype(BF16))
 
     features = features_ref[...].astype(F32).reshape(ROWS, LANES)
     f3 = features.reshape(BRICKS, 64, LANES)
@@ -332,22 +388,21 @@
     active = (before * sigmoid).astype(BF16)
     table[0:512, :] = active
 
-    grad = cotangent_ref[...].astype(F32).reshape(ROWS, LANES)
-    grad_b = grad.astype(BF16)
     pooled = fold_lanes(jnp.where(half_mask, dot(pool, active), 0.0)) * (1.0 / 64.0)
     grad_up = fold_lanes(jnp.where(half_mask, dot(pool, grad_b), 0.0))
     small = jnp.where(low_half, pooled, grad_up).astype(BF16)
-    i, j = spread_index((BRICKS, 128))
-    wide_embedding = jnp.concatenate([embedding, embedding], axis=1)
-    rounded = wide_embedding.astype(BF16).astype(F32)
-    rounded = jnp.where(j < 64, rounded, wide_embedding - rounded)
-    rounded = jnp.concatenate([jnp.zeros((8, 128), F32), rounded] * n_dev, axis=0)
-    small = dot_tn(hot_target, small) + rounded
+    wide = jnp.concatenate([embedding, embedding], axis=1)
+    wide = jnp.concatenate([jnp.zeros((8, 128), F32), wide] * n_dev, axis=0)
+    i, j = spread_index((n_dev * SLOT_ROWS, 128))
+    codes = jnp.where(j < 96, shift_rows(directions, 8), directions)
+    codes = jnp.where((i & 8) == 8, codes, 0.0)
+    small = dot_tn(hot_target, small) + jnp.where(j < 64, wide, codes)
     small_out[...] = small.astype(BF16).reshape(n_dev, SLOT_ROWS, 128)
     small_in[dev] = small_out[dev]
-    barrier = pltpu.get_barrier_semaphore()
-    pl.semaphore_wait(barrier, n_dev - 1 + n_grp - 1)
+
+    entry_wait()
     exchange(lambda p: small_out.at[p], small_in.at[dev], 0, "dev")
+    exchange(lambda p: layer_out.at[p], layer_in.at[dev], 2, "dev")
 
     z_first, z_last = z_table(active, y_mask, select_x)
     table[512:576, :] = z_first
@@ -356,7 +411,6 @@
         dot_tn(hot_out[...], table[...]).astype(BF16).reshape(n_dev, SLOT_ROWS, LANES)
     )
     face_in[dev] = face_out[dev]
-    exchange(lambda p: face_out.at[p], face_in.at[dev], 1, "dev")
 
     i, j = spread_index((64, LANES))
     wide = dot(fine_weight_ref[...].reshape(448, 64), one_hot(i == (j & 63)))
@@ -381,33 +435,11 @@
         ),
     ).astype(BF16)
 
-    i, j = spread_index((64, ROWS))
-    g4 = grad.reshape(BRICKS, 8, 8, LANES)
-    grad_z = z_table(grad_b, y_mask, select_x)
-    layers = [
-        g4[:, 0].reshape(64, LANES).astype(BF16),
-        g4[:, 7].reshape(64, LANES).astype(BF16),
-        dot(one_hot(j == i * 8), grad_b).astype(BF16),
-        dot(one_hot(j == i * 8 + 7), grad_b).astype(BF16),
-        grad_z[0],
-        grad_z[1],
-    ]
-    rims = []
-    for k in range(6):
+    def times_band(v, k):
         band = band_ref[256 * k : 256 * (k + 1), :]
-        rims.append(
-            jnp.concatenate(
-                [dot_nt(layers[k][:, 0:256], band), dot_nt(layers[k][:, 256:512], band)], axis=1
-            ).astype(BF16)
-        )
-    rim = jnp.concatenate(rims, axis=0)
-    rim_out[...] = (
-        dot(hot_halo[640 : 640 + n_dev * SLOT_ROWS, :], rim)
-        .astype(BF16)
-        .reshape(n_dev, SLOT_ROWS, LANES)
-    )
-    rim_in[dev] = rim_out[dev]
-    exchange(lambda p: rim_out.at[p], rim_in.at[dev], 2, "dev")
+        return jnp.concatenate([dot_nt(v[:, 0:256], band), dot_nt(v[:, 256:512], band)], axis=1)
+
+    rim = jnp.concatenate([times_band(layers[k], k).astype(BF16) for k in range(6)], axis=0)
 
     x_at, y_at = (row >> 3) & 7, row & 7
 
@@ -428,11 +460,35 @@
     grad_ref[...] = total
 
     active_f = active.astype(F32)
-    conv_ref[...] = dot(active, middle)
+    halo = dot_tn(hot_halo[0:640, :], table[...]).astype(BF16)
     grad_t = grad.T.astype(BF16)
     center = dot(grad_t, active)
-
-    wait_arrived(others(small_in, n_dev), 0, "dev")
+    conv = dot(active, middle)
+    left, right = conv[:, 0:256], conv[:, 256:512]
+    tap_grads = [diagonal_sum(center, 0, 0, 8)]
+    for k in range(4):
+        repeat = repeat_x if k < 2 else repeat_y
+        moved = shifted(active_f, k, dot(repeat, halo[64 * k : 64 * k + 64])).astype(BF16)
+        band = band_ref[256 * k : 256 * (k + 1), :]
+        left = left + dot(moved[:, 0:256], band)
+        right = right + dot(moved[:, 256:512], band)
+        tap_grads.append(
+            diagonal_sum(dot(grad_t[0:256], moved[:, 0:256]), 0, 0, 4)
+            + diagonal_sum(dot(grad_t[256:512], moved[:, 256:512]), 0, 0, 4)
+        )
+    low_z = jnp.where(y_mask, dot(repeat_y, halo[256:320]), 0.0).astype(BF16)
+    high_z = jnp.where(y_mask, dot(repeat_y, halo[320:384]), 0.0).astype(BF16)
+    end = jnp.where(low_half, weight_ref[320:384, 0:128], 0.0).astype(BF16)
+    first = dot(low_z, jnp.concatenate([end] * 8, axis=0))
+    end = jnp.where(low_half, 0.0, weight_ref[384:448, 0:128]).astype(BF16)
+    last = dot(high_z, jnp.concatenate([end] * 8, axis=0))
+    conv_ref[...] = jnp.concatenate(
+        [left[:, 0:128] + first, left[:, 128:256], right[:, 0:128], right[:, 128:256] + last],
+        axis=1,
+    )
+    tap_grads.append(diagonal_sum(center, 0, -1, 8) + fold_lanes(dot(grad_t[0:64], low_z)))
+    tap_grads.append(diagonal_sum(center, 0, 1, 8) + fold_lanes(dot(grad_t[448:512], high_z)))
+
     place = exact_dot(places_ref[...].astype(F32), spread_slot)
     j = iota((1, n_dev * SLOT_ROWS), 1)
     place_code = (place * 8 + (j & 7).astype(F32)).astype(jnp.int32)
@@ -446,6 +502,7 @@
     first_kind = (j & 8) == 0
     hot_place = one_hot(voxel_code == jnp.where(first_kind, place_code, -1))
     hot_place_grad = one_hot(voxel_code == jnp.where(first_kind, -1, place_code))
+    wait_arrived(others(small_in, n_dev), 0, "dev")
     grid = dot(hot_place, small_in[...].reshape(n_dev * SLOT_ROWS, 128)).astype(BF16)
     down = jnp.concatenate([down_weight_ref[...], jnp.zeros((64, 128), BF16)], axis=0)
     up = jnp.concatenate([jnp.zeros((64, 128), BF16), up_weight_ref[...]], axis=0)
@@ -483,34 +540,33 @@
     )
     back_in[dev] = back_out[dev]
     exchange(lambda p: back_out.at[p], back_in.at[dev], 3, "dev")
+
     coarse_grad = dot_tn(stack, grad_out_b)
     down_grad = dot_tn(grid, grad_pre)
     up_grad = dot_tn(grid, coarse_out)
-
     part = jnp.concatenate([coarse_grad, down_grad[0:64], up_grad[64:128]], axis=0)
-    pair_out[...] = part.astype(BF16).reshape(2, COARSE_ROWS // 2, 128)
-    exchange(lambda p: pair_out.at[p], pair_in, 4, "core")
-
-    wait_arrived(others(face_in, n_dev), 1, "dev")
-    halo = dot_tn(hot_halo[0:640, :], table[...]) + dot_tn(
-        hot_halo[640 : 640 + n_dev * SLOT_ROWS, :],
-        face_in[...].reshape(n_dev * SLOT_ROWS, LANES),
-    )
-    halo = halo.astype(BF16)
-    tap_grads = [diagonal_sum(center, 0, 0, 8)]
-    taps = []
-    for k in range(4):
-        repeat = repeat_x if k < 2 else repeat_y
-        moved = shifted(active_f, k, dot(repeat, halo[64 * k : 64 * k + 64])).astype(BF16)
-        taps.append(moved)
-        tap_grads.append(
-            diagonal_sum(dot(grad_t[0:256], moved[:, 0:256]), 0, 0, 4)
-            + diagonal_sum(dot(grad_t[256:512], moved[:, 256:512]), 0, 0, 4)
+    coarse_part[...] = part.astype(BF16).reshape(2 * n_grp, coarse_chunk, 128)
+    plane = rings["plane"][0]
+    coarse_in[plane] = coarse_part[plane]
+    exchange(lambda p: coarse_part.at[p], coarse_in.at[plane], 4, "plane")
+
+    exchange(lambda p: face_out.at[p], face_in.at[dev], 1, "dev")
+
+    wait_arrived(others(layer_in, n_dev), 2, "dev")
+    came = layer_in[...].reshape(n_dev * SLOT_ROWS, LANES)
+    came_f = came.astype(F32)
+    came_t = came_f.T.astype(BF16)
+    faces = face_out[...].reshape(n_dev * SLOT_ROWS, LANES).astype(F32)
+    marks = small_in[...].reshape(n_dev * SLOT_ROWS, 128).astype(F32)
+    odd_slot = (iota((n_dev * SLOT_ROWS, 1), 0) & 8) == 8
+    way = jnp.where(odd_slot, marks[:, 96:97], shift_rows(marks, -8)[:, 64:65])
+    for k in range(6):
+        own_faces = jnp.where(way == float(k), faces, 0.0).astype(BF16)
+        tap_grads[k + 1] = (
+            tap_grads[k + 1]
+            + diagonal_sum(dot(came_t[0:256], own_faces[:, 0:256]), 0, 0, 4)
+            + diagonal_sum(dot(came_t[256:512], own_faces[:, 256:512]), 0, 0, 4)
         )
-    low_z = jnp.where(y_mask, dot(repeat_y, halo[256:320]), 0.0).astype(BF16)
-    high_z = jnp.where(y_mask, dot(repeat_y, halo[320:384]), 0.0).astype(BF16)
-    tap_grads.append(diagonal_sum(center, 0, -1, 8) + fold_lanes(dot(grad_t[0:64], low_z)))
-    tap_grads.append(diagonal_sum(center, 0, 1, 8) + fold_lanes(dot(grad_t[448:512], high_z)))
     fine_rows = []
     for t in range(4):
         low = tap_grads[t].T[0:64]
@@ -519,63 +575,20 @@
     part = jnp.concatenate(fine_rows, axis=0)
     fine_out[...] = part.astype(BF16).reshape(n_grp, FINE_ROWS // n_grp, 128)
     fine_in[grp] = fine_out[grp]
-    exchange(lambda p: fine_out.at[p], fine_in.at[grp], 9, "grp")
-
-    wait_arrived(pair_in, 4, "core")
-    part = pair_out[core].astype(F32) + pair_in[...].astype(F32)
-    coarse_out_ref[...] = part.astype(BF16).reshape(n_grp, COARSE_ROWS // 2 // n_grp, 128)
-    coarse_in[grp] = coarse_out_ref[grp]
-    exchange(lambda p: coarse_out_ref.at[p], coarse_in.at[grp], 5, "grp")
-
-    conv = conv_ref[...]
-    left, right = conv[:, 0:256], conv[:, 256:512]
-    for k in range(4):
-        band = band_ref[256 * k : 256 * (k + 1), :]
-        left = left + dot(taps[k][:, 0:256], band)
-        right = right + dot(taps[k][:, 256:512], band)
-    end = jnp.where(low_half, weight_ref[320:384, 0:128], 0.0).astype(BF16)
-    first = dot(low_z, jnp.concatenate([end] * 8, axis=0))
-    end = jnp.where(low_half, 0.0, weight_ref[384:448, 0:128]).astype(BF16)
-    last = dot(high_z, jnp.concatenate([end] * 8, axis=0))
-    conv_ref[...] = jnp.concatenate(
-        [left[:, 0:128] + first, left[:, 128:256], right[:, 0:128], right[:, 128:256] + last],
-        axis=1,
-    )
-
-    wait_arrived(others(coarse_in, n_grp), 5, "grp")
-    part = coarse_in[0].astype(F32)
-    for p in range(1, n_grp):
-        part = part + coarse_in[p].astype(F32)
-    coarse_mid[chip] = part.astype(BF16)
-    exchange(lambda p: coarse_mid.at[chip], coarse_mid.at[chip], 6, "chip")
-
-    wait_arrived(others(back_in, n_dev), 3, "dev")
-    back = back_in[...].reshape(n_dev * SLOT_ROWS, 128)
-    coarse_values = dot(hot_target, back).astype(BF16)
-    i, j = spread_index((64, LANES))
-    up_wide = dot_tn(up_weight_ref[...], one_hot(i == (j & 63))).astype(BF16)
-    upward = jnp.where(half_mask, dot(coarse_values, up_wide), 0.0)
-    upward_high = upward.astype(BF16)
-    upward_low = (upward - upward_high.astype(F32)).astype(BF16)
-    upward = dot(unpool, upward_high) + dot(unpool, upward_low)
-    features = features_ref[...].astype(F32).reshape(ROWS, LANES)
-    mixed = features + conv_ref[...] + upward
-    mixed_held[...] = mixed.reshape(BRICKS, 8, 8, LANES).astype(BF16)
-    mixed_copy = pltpu.make_async_copy(mixed_held, mixed_ref, copy_sems.at[0])
-    mixed_copy.start()
-
-    back_grad = dot(hot_target_grad, back).astype(BF16)
-    i, j = spread_index((128, LANES))
-    back_wide = jnp.where(half_mask, dot(back_grad, one_hot(i == (j & 63))), 0.0)
-    total = grad_ref[...] + dot(unpool, (back_wide * (1.0 / 64.0)).astype(BF16))
-    wait_arrived(others(rim_in, n_dev), 2, "dev")
-    rim_back = rim_in[...].reshape(n_dev * SLOT_ROWS, LANES)
-    total = total + dot(hot_out[0:512, :], rim_back)
+    exchange(lambda p: fine_out.at[p], fine_in.at[grp], 7, "grp")
+
+    rim_back = jnp.zeros((n_dev * SLOT_ROWS, LANES), F32)
+    for k in range(6):
+        rim_back = rim_back + times_band(
+            jnp.where(way == float(k), came_f, 0.0).astype(BF16), k
+        )
+    rim_back = rim_back.astype(BF16)
+    total = grad_ref[...] + dot(hot_out[0:512, :], rim_back)
     z_rows = (z_rows + dot(hot_out[512:640, :], rim_back)).astype(BF16)
     low_rows = lane[:, 0:128] < 64
     first = fold_lanes(jnp.where(y_mask, dot(repeat_y, z_rows[0:64]), 0.0))
     last = fold_lanes(jnp.where(y_mask, dot(repeat_y, z_rows[64:128]), 0.0))
-    total = jnp.concatenate(
+    grad_ref[...] = jnp.concatenate(
         [
             total[:, 0:128] + jnp.where(low_rows, first, 0.0),
             total[:, 128:384],
@@ -583,27 +596,34 @@
         ],
         axis=1,
     )
+
+    wait_arrived(others(coarse_in, 2 * n_grp), 4, "plane")
+    part = coarse_in[0].astype(F32)
+    for p in range(1, 2 * n_grp):
+        part = part + coarse_in[p].astype(F32)
+    coarse_mid[chip] = part.astype(BF16)
+    exchange(lambda p: coarse_mid.at[chip], coarse_mid.at[chip], 5, "chip")
+
+    wait_arrived(others(back_in, n_dev), 3, "dev")
+    back = back_in[...].reshape(n_dev * SLOT_ROWS, 128)
+    back_grad = dot(hot_target_grad, back).astype(BF16)
+    i, j = spread_index((128, LANES))
+    back_wide = jnp.where(half_mask, dot(back_grad, one_hot(i == (j & 63))), 0.0)
+    total = grad_ref[...] + dot(unpool, (back_wide * (1.0 / 64.0)).astype(BF16))
     normed = normed_ref[...]
     grad_before = total * slope_ref[...]
     grad_ref[...] = grad_before
     grad_scale = fold_lanes(brick_sum(grad_before * normed))
     grad_shift = fold_lanes(brick_sum(grad_before))
     brick_all[dev] = jnp.where(low_b, grad_scale, grad_shift)
-    exchange(lambda p: brick_all.at[dev], brick_all.at[dev], 11, "dev")
-
-    wait_arrived(others(fine_in, n_grp), 9, "grp")
+    exchange(lambda p: brick_all.at[dev], brick_all.at[dev], 9, "dev")
+
+    wait_arrived(others(fine_in, n_grp), 7, "grp")
     part = fine_in[0].astype(F32)
     for p in range(1, n_grp):
         part = part + fine_in[p].astype(F32)
     fine_mid[dev] = part.astype(BF16)
-    exchange(lambda p: fine_mid.at[dev], fine_mid.at[dev], 10, "dev")
-
-    wait_arrived(others(coarse_mid, n_chip), 6, "chip")
-    part = coarse_mid[0].astype(F32)
-    for p in range(1, n_chip):
-        part = part + coarse_mid[p].astype(F32)
-    coarse_all[core, grp] = part.astype(BF16)
-    exchange(lambda p: coarse_all.at[core, grp], coarse_all.at[core, grp], 7, "grp")
+    exchange(lambda p: fine_mid.at[dev], fine_mid.at[dev], 8, "dev")
 
     grad_before = grad_ref[...]
     g3 = grad_before.reshape(BRICKS, 64, LANES) * per_brick(gain)
@@ -617,16 +637,36 @@
     input_grad_copy = pltpu.make_async_copy(input_grad_held, input_grad_ref, copy_sems.at[1])
     input_grad_copy.start()
 
-    wait_arrived(others(fine_mid, n_dev), 10, "dev")
-    part = fine_mid[0].astype(F32)
-    for p in range(1, n_dev):
-        part = part + fine_mid[p].astype(F32)
-    fine_all[grp] = part.astype(BF16)
-    exchange(lambda p: fine_all.at[grp], fine_all.at[grp], 12, "grp")
-
-    wait_arrived(others(brick_all, n_dev), 11, "dev")
+    coarse_values = dot(hot_target, back).astype(BF16)
+    i, j = spread_index((64, LANES))
+    up_wide = dot_tn(up_weight_ref[...], one_hot(i == (j & 63))).astype(BF16)
+    upward = jnp.where(half_mask, dot(coarse_values, up_wide), 0.0)
+    upward_high = upward.astype(BF16)
+    upward_low = (upward - upward_high.astype(F32)).astype(BF16)
+    upward = dot(unpool, upward_high) + dot(unpool, upward_low)
+    features = features_ref[...].astype(F32).reshape(ROWS, LANES)
+    conv_ref[...] = features + conv_ref[...] + upward
+    i, j = spread_index((ROWS, 256))
+    x, y = (i >> 3) & 7, i & 7
+    by_x = (j & 63) == ((i >> 6) * 8 + y)
+    by_y = (j & 63) == (i >> 3)
+    way = j >> 6
+    edges = one_hot(
+        ((way == 0) & (x == 0) & by_x)
+        | ((way == 1) & (x == 7) & by_x)
+        | ((way == 2) & (y == 0) & by_y)
+        | ((way == 3) & (y == 7) & by_y)
+    )
+
+    wait_arrived(others(coarse_mid, n_chip), 5, "chip")
+    part = coarse_mid[0].astype(F32)
+    for p in range(1, n_chip):
+        part = part + coarse_mid[p].astype(F32)
+    coarse_all[plane] = part.astype(BF16)
+    exchange(lambda p: coarse_all.at[plane], coarse_all.at[plane], 6, "plane")
+
+    wait_arrived(others(brick_all, n_dev), 9, "dev")
     embeddings = small_in[...].astype(F32)[:, 8:16, :].reshape(n_dev * BRICKS, 128)
-    embeddings = embeddings + pltpu.roll(embeddings, 64, 1)
     time_grad = lax.dot_general(
         embeddings,
         brick_all[...].reshape(n_dev * BRICKS, 128),
@@ -635,15 +675,46 @@
         preferred_element_type=F32,
     )
     time_all[grp] = time_grad[0:64].astype(BF16)
-    exchange(lambda p: time_all.at[grp], time_all.at[grp], 13, "grp")
-
-    wait_arrived(others(coarse_all.at[0], n_grp), 7, "grp")
-    exchange(lambda p: coarse_all.at[core], coarse_all.at[core], 8, "core")
-    wait_arrived(others(fine_all, n_grp), 12, "grp")
+    exchange(lambda p: time_all.at[grp], time_all.at[grp], 11, "grp")
+
+    wait_arrived(others(fine_mid, n_dev), 8, "dev")
+    part = fine_mid[0].astype(F32)
+    for p in range(1, n_dev):
+        part = part + fine_mid[p].astype(F32)
+    fine_all[grp] = part.astype(BF16)
+    exchange(lambda p: fine_all.at[grp], fine_all.at[grp], 10, "grp")
+
+    wait_arrived(others(face_in, n_dev), 1, "dev")
+    halo = dot_tn(hot_halo[640 : 640 + n_dev * SLOT_ROWS, :], face_in[...].reshape(-1, LANES))
+    halo = halo.astype(BF16)
+    sides = []
+    for k in range(6):
+        band = band_ref[256 * k : 256 * (k + 1), :]
+        piece = halo[64 * k : 64 * k + 64]
+        sides.append(
+            jnp.concatenate([dot(piece[:, 0:256], band), dot(piece[:, 256:512], band)], axis=1)
+            .astype(BF16)
+        )
+    mixed = conv_ref[...] + dot(edges, jnp.concatenate(sides[0:4], axis=0))
+    first = fold_lanes(jnp.where(y_mask, dot(repeat_y, sides[4]), 0.0))
+    last = fold_lanes(jnp.where(y_mask, dot(repeat_y, sides[5]), 0.0))
+    mixed = jnp.concatenate(
+        [
+            mixed[:, 0:128] + jnp.where(low_rows, first, 0.0),
+            mixed[:, 128:384],
+            mixed[:, 384:512] + jnp.where(low_rows, 0.0, last),
+        ],
+        axis=1,
+    )
+    mixed_held[...] = mixed.reshape(BRICKS, 8, 8, LANES).astype(BF16)
+    mixed_copy = pltpu.make_async_copy(mixed_held, mixed_ref, copy_sems.at[0])
+    mixed_copy.start()
+
+    wait_arrived(others(coarse_all, 2 * n_grp), 6, "plane")
+    coarse_sum_ref[...] = coarse_all[...].reshape(COARSE_ROWS, 128)
+    wait_arrived(others(fine_all, n_grp), 10, "grp")
     fine_sum_ref[...] = fine_all[...].reshape(FINE_ROWS, 128)
-    wait_arrived(coarse_all.at[0], 8, "core")
-    coarse_sum_ref[...] = coarse_all[...].reshape(COARSE_ROWS, 128)
-    wait_arrived(others(time_all, n_grp), 13, "grp")
+    wait_arrived(others(time_all, n_grp), 11, "grp")
     part = time_all[0].astype(F32)
     for p in range(1, n_grp):
         part = part + time_all[p].astype(F32)
@@ -651,18 +722,16 @@
 
     wait_sent(others(small_out, n_dev), 0, "dev")
     wait_sent(others(face_out, n_dev), 1, "dev")
-    wait_sent(others(rim_out, n_dev), 2, "dev")
+    wait_sent(others(layer_out, n_dev), 2, "dev")
     wait_sent(others(back_out, n_dev), 3, "dev")
-    wait_sent(pair_in, 4, "core")
-    wait_sent(others(coarse_out_ref, n_grp), 5, "grp")
-    wait_sent(others(coarse_mid, n_chip), 6, "chip")
-    wait_sent(others(coarse_all.at[0], n_grp), 7, "grp")
-    wait_sent(coarse_all.at[0], 8, "core")
-    wait_sent(others(fine_out, n_grp), 9, "grp")
-    wait_sent(others(fine_mid, n_dev), 10, "dev")
-    wait_sent(others(brick_all, n_dev), 11, "dev")
-    wait_sent(others(fine_all, n_grp), 12, "grp")
-    wait_sent(others(time_all, n_grp), 13, "grp")
+    wait_sent(others(coarse_part, 2 * n_grp), 4, "plane")
+    wait_sent(others(coarse_mid, n_chip), 5, "chip")
+    wait_sent(others(coarse_all, 2 * n_grp), 6, "plane")
+    wait_sent(others(fine_out, n_grp), 7, "grp")
+    wait_sent(others(fine_mid, n_dev), 8, "dev")
+    wait_sent(others(brick_all, n_dev), 9, "dev")
+    wait_sent(others(fine_all, n_grp), 10, "grp")
+    wait_sent(others(time_all, n_grp), 11, "grp")
     mixed_copy.wait()
     input_grad_copy.wait()
 
@@ -702,12 +771,12 @@
     args[4] = jnp.swapaxes(args[4], 1, 2)
     args[6] = args[6].reshape(1, n_dev)
     args[11] = args[11].T
+    args.append(frequency)
     vmem = pl.BlockSpec(memory_space=pltpu.VMEM)
     free = pl.BlockSpec(memory_space=pl.ANY)
     packed = jax.ShapeDtypeStruct((BRICKS, 8, 8, LANES), BF16)
     slots = (n_dev, SLOT_ROWS)
-    coarse_half = COARSE_ROWS // 2
-    coarse_chunk = coarse_half // n_grp
+    coarse_chunk = COARSE_ROWS // 2 // n_grp
     fine_chunk = FINE_ROWS // n_grp
     held = pl.pallas_call(
         functools.partial(kernel, n_grp, n_dev),
@@ -718,7 +787,7 @@
             jax.ShapeDtypeStruct((FINE_ROWS, 128), BF16),
             jax.ShapeDtypeStruct((64, 128), F32),
         ),
-        in_specs=[vmem] * 13,
+        in_specs=[free] * 13,
         out_specs=(free, free, vmem, vmem, vmem),
         scratch_shapes=[
             pltpu.VMEM(slots + (128,), BF16),
@@ -729,12 +798,10 @@
             pltpu.VMEM(slots + (LANES,), BF16),
             pltpu.VMEM(slots + (128,), BF16),
             pltpu.VMEM(slots + (128,), BF16),
-            pltpu.VMEM((2, coarse_half, 128), BF16),
-            pltpu.VMEM((coarse_half, 128), BF16),
-            pltpu.VMEM((n_grp, coarse_chunk, 128), BF16),
-            pltpu.VMEM((n_grp, coarse_chunk, 128), BF16),
+            pltpu.VMEM((2 * n_grp, coarse_chunk, 128), BF16),
+            pltpu.VMEM((2 * n_grp, coarse_chunk, 128), BF16),
             pltpu.VMEM((n_dev // 2, coarse_chunk, 128), BF16),
-            pltpu.VMEM((2, n_grp, coarse_chunk, 128), BF16),
+            pltpu.VMEM((2 * n_grp, coarse_chunk, 128), BF16),
             pltpu.VMEM((n_grp, fine_chunk, 128), BF16),
             pltpu.VMEM((n_grp, fine_chunk, 128), BF16),
             pltpu.VMEM((n_dev, fine_chunk, 128), BF16),
@@ -752,14 +819,16 @@
             pltpu.VMEM((ROWS, LANES), F32),
             pltpu.VMEM((448, LANES), F32),
             pltpu.VMEM((1536, 256), BF16),
-            pltpu.SemaphoreType.DMA((14,)),
-            pltpu.SemaphoreType.DMA((14,)),
+            pltpu.SemaphoreType.DMA((12,)),
+            pltpu.SemaphoreType.DMA((12,)),
             pltpu.SemaphoreType.DMA((2,)),
-        ],
+        ]
+        + [pltpu.VMEM(a.shape, a.dtype) for a in args]
+        + [pltpu.SemaphoreType.DMA((13,))],
         compiler_params=pltpu.CompilerParams(
             collective_id=0, has_side_effects=True, vmem_limit_bytes=56 * 1024 * 1024
         ),
-    )(*args, frequency)
+    )(*args)
     outs = pl.pallas_call(
         finish,
         out_shape=(

time: 50.7 us -> 47.3 us (0.933)
  Pallas kernels: 49.9 us -> 46.5 us
    pallas_call x1, Pallas kernels: 47.4 us -> 43.9 us  [body(): pl.pallas_call(functools.partial(kernel, n_grp, n_dev), out_shape=(packed...]
where the time goes in v3:
time: 47.3 us; the launch traced here: 47.1 us
  Pallas kernels  46.5 us (98%)
  between operations  0.65 us (1%)
    pallas_call x1, Pallas kernels, body(): pl.pallas_call(functools.partial(kernel, n_grp, n_dev), out_shape=(packed...  43.9 us
    pallas_call x1, Pallas kernels, body(): pl.pallas_call(finish, out_shape=(packed, packed, jax.ShapeDtypeStruct((7...  2.54 us

profile of v3, /device:TPU:1, one launch (start us, length us, event | category | flops | bytes accessed | tf_op | source)
XLA Modules:
  0.0 47.1 jit_solution(9345245004414092404)
XLA Ops:
  0.6 43.9 %shard_map.180 = (bf16[8,8,8,512]{3,2,1,0:T(8,128)(2,1)}, bf16[8,8,8,512]{3,2,1,0:T(8,128)(2,1)}, bf16[1024,128]{1,0:T(8,128)(2,1)}, bf16[256,128]{1,0:T(8,128)(2,1)}, f32[64,128]{1,0:T(8,128)}) custom-call(bf16[8,8,8,512]{3,2,1,0:T(8,128)(2,1)} %features_far.1, bf16[8,8,8,512]{3,2,1,0:T(8,128)(2,1)} %cotangent_far.1, s32[8]{0:T(128)} %steps_far.1, ...), custom_call_target="tpu_custom_call" | custom-call | tf_op jit(solution)/shard_map/pallas_call | solution.py:781
  44.6 2.5 %shard_map.181 = (bf16[8,8,8,512]{3,2,1,0:T(8,128)(2,1)}, bf16[8,8,8,512]{3,2,1,0:T(8,128)(2,1)}, f32[7,64,64]{2,1,0:T(8,128)}, f32[64,128]{1,0:T(8,128)}, f32[7...) custom-call(bf16[8,8,8,512]{3,2,1,0:T(8,128)(2,1)} %get-tuple-element.19.mixed_in, ...), custom_call_target="tpu_custom_call" | custom-call | tf_op jit(solution)/shard_map/pallas_call | solution.py:832

commit v4 on v3

--- a/solution.py
+++ b/solution.py
@@ -151,6 +151,7 @@
     time_all,
     mixed_held,
     input_grad_held,
+    own_faces,
     hot_halo,
     hot_out,
     table,
@@ -552,36 +553,37 @@
 
     exchange(lambda p: face_out.at[p], face_in.at[dev], 1, "dev")
 
-    wait_arrived(others(layer_in, n_dev), 2, "dev")
-    came = layer_in[...].reshape(n_dev * SLOT_ROWS, LANES)
-    came_f = came.astype(F32)
-    came_t = came_f.T.astype(BF16)
-    faces = face_out[...].reshape(n_dev * SLOT_ROWS, LANES).astype(F32)
     marks = small_in[...].reshape(n_dev * SLOT_ROWS, 128).astype(F32)
     odd_slot = (iota((n_dev * SLOT_ROWS, 1), 0) & 8) == 8
     way = jnp.where(odd_slot, marks[:, 96:97], shift_rows(marks, -8)[:, 64:65])
+    way_row = jnp.broadcast_to(way, (n_dev * SLOT_ROWS, 128)).T[0:1]
+    faces_t = face_out[...].reshape(n_dev * SLOT_ROWS, LANES).astype(F32).T
     for k in range(6):
-        own_faces = jnp.where(way == float(k), faces, 0.0).astype(BF16)
+        own_faces[LANES * k : LANES * (k + 1), :] = jnp.where(
+            way_row == float(k), faces_t, 0.0
+        ).astype(BF16)
+    tap_grads = [jnp.concatenate([t, t], axis=0).T[0:64] for t in tap_grads]
+    wait_arrived(others(layer_in, n_dev), 2, "dev")
+    came = layer_in[...].reshape(n_dev * SLOT_ROWS, LANES)
+    for k in range(6):
+        base = LANES * k
         tap_grads[k + 1] = (
             tap_grads[k + 1]
-            + diagonal_sum(dot(came_t[0:256], own_faces[:, 0:256]), 0, 0, 4)
-            + diagonal_sum(dot(came_t[256:512], own_faces[:, 256:512]), 0, 0, 4)
+            + diagonal_sum(dot(own_faces[base : base + 256, :], came[:, 0:256]), 0, 0, 4)
+            + diagonal_sum(dot(own_faces[base + 256 : base + 512, :], came[:, 256:512]), 0, 0, 4)
         )
     fine_rows = []
     for t in range(4):
-        low = tap_grads[t].T[0:64]
-        high = tap_grads[t + 4].T[0:64] if t < 3 else jnp.zeros_like(low)
-        fine_rows.append(jnp.concatenate([low, high], axis=1))
+        high = pltpu.roll(tap_grads[t + 4], 64, 1) if t < 3 else 0.0
+        fine_rows.append(jnp.where(low_half, tap_grads[t], high))
     part = jnp.concatenate(fine_rows, axis=0)
     fine_out[...] = part.astype(BF16).reshape(n_grp, FINE_ROWS // n_grp, 128)
     fine_in[grp] = fine_out[grp]
     exchange(lambda p: fine_out.at[p], fine_in.at[grp], 7, "grp")
 
-    rim_back = jnp.zeros((n_dev * SLOT_ROWS, LANES), F32)
-    for k in range(6):
-        rim_back = rim_back + times_band(
-            jnp.where(way == float(k), came_f, 0.0).astype(BF16), k
-        )
+    rim_back = times_band(came, 0)
+    for k in range(1, 6):
+        rim_back = jnp.where(way == float(k), times_band(came, k), rim_back)
     rim_back = rim_back.astype(BF16)
     total = grad_ref[...] + dot(hot_out[0:512, :], rim_back)
     z_rows = (z_rows + dot(hot_out[512:640, :], rim_back)).astype(BF16)
@@ -636,6 +638,13 @@
     input_grad_held[...] = result.reshape(BRICKS, 8, 8, LANES).astype(BF16)
     input_grad_copy = pltpu.make_async_copy(input_grad_held, input_grad_ref, copy_sems.at[1])
     input_grad_copy.start()
+
+    wait_arrived(others(coarse_mid, n_chip), 5, "chip")
+    part = coarse_mid[0].astype(F32)
+    for p in range(1, n_chip):
+        part = part + coarse_mid[p].astype(F32)
+    coarse_all[plane] = part.astype(BF16)
+    exchange(lambda p: coarse_all.at[plane], coarse_all.at[plane], 6, "plane")
 
     coarse_values = dot(hot_target, back).astype(BF16)
     i, j = spread_index((64, LANES))
@@ -657,13 +666,6 @@
         | ((way == 2) & (y == 0) & by_y)
         | ((way == 3) & (y == 7) & by_y)
     )
-
-    wait_arrived(others(coarse_mid, n_chip), 5, "chip")
-    part = coarse_mid[0].astype(F32)
-    for p in range(1, n_chip):
-        part = part + coarse_mid[p].astype(F32)
-    coarse_all[plane] = part.astype(BF16)
-    exchange(lambda p: coarse_all.at[plane], coarse_all.at[plane], 6, "plane")
 
     wait_arrived(others(brick_all, n_dev), 9, "dev")
     embeddings = small_in[...].astype(F32)[:, 8:16, :].reshape(n_dev * BRICKS, 128)
@@ -810,6 +812,7 @@
             pltpu.VMEM((n_grp, 64, 128), BF16),
             pltpu.VMEM((BRICKS, 8, 8, LANES), BF16),
             pltpu.VMEM((BRICKS, 8, 8, LANES), BF16),
+            pltpu.VMEM((6 * LANES, n_dev * SLOT_ROWS), BF16),
             pltpu.VMEM((640 + n_dev * SLOT_ROWS, 384), BF16),
             pltpu.VMEM((640, n_dev * SLOT_ROWS), BF16),
             pltpu.VMEM((640, LANES), BF16),

time: 47.3 us -> 45.8 us (0.968)
  Pallas kernels: 46.5 us -> 45.1 us
    pallas_call x1, Pallas kernels: 43.9 us -> 42.5 us  [body(): pl.pallas_call(functools.partial(kernel, n_grp, n_dev), out_shape=(packed...]
where the time goes in v4:
time: 45.8 us; the launch traced here: 45.7 us
  Pallas kernels  45.1 us (98%)
  between operations  0.65 us (1%)
    pallas_call x1, Pallas kernels, body(): pl.pallas_call(functools.partial(kernel, n_grp, n_dev), out_shape=(packed...  42.5 us
    pallas_call x1, Pallas kernels, body(): pl.pallas_call(finish, out_shape=(packed, packed, jax.ShapeDtypeStruct((7...  2.54 us

profile of v4, /device:TPU:1, one launch (start us, length us, event | category | flops | bytes accessed | tf_op | source)
XLA Modules:
  0.0 45.7 jit_solution(4777281900016487016)
XLA Ops:
  0.6 42.5 %shard_map.180 = (bf16[8,8,8,512]{3,2,1,0:T(8,128)(2,1)}, bf16[8,8,8,512]{3,2,1,0:T(8,128)(2,1)}, bf16[1024,128]{1,0:T(8,128)(2,1)}, bf16[256,128]{1,0:T(8,128)(2,1)}, f32[64,128]{1,0:T(8,128)}) custom-call(bf16[8,8,8,512]{3,2,1,0:T(8,128)(2,1)} %features_far.1, bf16[8,8,8,512]{3,2,1,0:T(8,128)(2,1)} %cotangent_far.1, s32[8]{0:T(128)} %steps_far.1, ...), custom_call_target="tpu_custom_call" | custom-call | tf_op jit(solution)/shard_map/pallas_call | solution.py:783
  43.2 2.5 %shard_map.181 = (bf16[8,8,8,512]{3,2,1,0:T(8,128)(2,1)}, bf16[8,8,8,512]{3,2,1,0:T(8,128)(2,1)}, f32[7,64,64]{2,1,0:T(8,128)}, f32[64,128]{1,0:T(8,128)}, f32[7...) custom-call(bf16[8,8,8,512]{3,2,1,0:T(8,128)(2,1)} %get-tuple-element.19.mixed_in, ...), custom_call_target="tpu_custom_call" | custom-call | tf_op jit(solution)/shard_map/pallas_call | solution.py:835

commit v5 on v4

--- a/solution.py
+++ b/solution.py
@@ -341,7 +341,7 @@
     repeat_x = one_hot(j == ((i >> 6) * 8 + (i & 7)))
     low_half = iota((64, 128), 1) < 64
 
-    grad = cotangent_ref[...].astype(F32).reshape(ROWS, LANES)
+    grad = cotangent_ref[...].astype(F32)
     grad_b = grad.astype(BF16)
     i, j = spread_index((64, ROWS))
     g4 = grad.reshape(BRICKS, 8, 8, LANES)
@@ -363,7 +363,7 @@
     layer_in[dev] = layer_out[dev]
     directions = dot(hot_slots, (iota((384, 128), 0) >> 6).astype(F32).astype(BF16))
 
-    features = features_ref[...].astype(F32).reshape(ROWS, LANES)
+    features = features_ref[...].astype(F32)
     f3 = features.reshape(BRICKS, 64, LANES)
     centred = f3 - per_brick(group_mean(jnp.sum(f3, axis=1)))
     variance = group_mean(jnp.sum(centred * centred, axis=1))
@@ -633,9 +633,9 @@
     mean_g = group_mean(jnp.sum(g3, axis=1))
     mean_gn = group_mean(jnp.sum(g3 * n3, axis=1))
     result = per_brick(inverse) * (g3 - per_brick(mean_g) - n3 * per_brick(mean_gn))
-    grad = cotangent_ref[...].astype(F32).reshape(ROWS, LANES)
+    grad = cotangent_ref[...].astype(F32)
     result = grad + result.reshape(ROWS, LANES)
-    input_grad_held[...] = result.reshape(BRICKS, 8, 8, LANES).astype(BF16)
+    input_grad_held[...] = result.astype(BF16)
     input_grad_copy = pltpu.make_async_copy(input_grad_held, input_grad_ref, copy_sems.at[1])
     input_grad_copy.start()
 
@@ -653,7 +653,7 @@
     upward_high = upward.astype(BF16)
     upward_low = (upward - upward_high.astype(F32)).astype(BF16)
     upward = dot(unpool, upward_high) + dot(unpool, upward_low)
-    features = features_ref[...].astype(F32).reshape(ROWS, LANES)
+    features = features_ref[...].astype(F32)
     conv_ref[...] = features + conv_ref[...] + upward
     i, j = spread_index((ROWS, 256))
     x, y = (i >> 3) & 7, i & 7
@@ -708,7 +708,7 @@
         ],
         axis=1,
     )
-    mixed_held[...] = mixed.reshape(BRICKS, 8, 8, LANES).astype(BF16)
+    mixed_held[...] = mixed.astype(BF16)
     mixed_copy = pltpu.make_async_copy(mixed_held, mixed_ref, copy_sems.at[0])
     mixed_copy.start()
 
@@ -770,13 +770,16 @@
     frequency = np.exp(-math.log(10000.0) * np.arange(half) / half).astype(np.float32)
     frequency = jnp.asarray(np.concatenate([frequency, frequency])[None, :])
     args = list(args)
+    whole = args[0].shape
+    args[0] = args[0].reshape(ROWS, LANES)
+    args[1] = args[1].reshape(ROWS, LANES)
     args[4] = jnp.swapaxes(args[4], 1, 2)
     args[6] = args[6].reshape(1, n_dev)
     args[11] = args[11].T
     args.append(frequency)
     vmem = pl.BlockSpec(memory_space=pltpu.VMEM)
     free = pl.BlockSpec(memory_space=pl.ANY)
-    packed = jax.ShapeDtypeStruct((BRICKS, 8, 8, LANES), BF16)
+    packed = jax.ShapeDtypeStruct((ROWS, LANES), BF16)
     slots = (n_dev, SLOT_ROWS)
     coarse_chunk = COARSE_ROWS // 2 // n_grp
     fine_chunk = FINE_ROWS // n_grp
@@ -810,8 +813,8 @@
             pltpu.VMEM((n_grp, fine_chunk, 128), BF16),
             pltpu.VMEM((n_dev, BRICKS, 128), F32),
             pltpu.VMEM((n_grp, 64, 128), BF16),
-            pltpu.VMEM((BRICKS, 8, 8, LANES), BF16),
-            pltpu.VMEM((BRICKS, 8, 8, LANES), BF16),
+            pltpu.VMEM((ROWS, LANES), BF16),
+            pltpu.VMEM((ROWS, LANES), BF16),
             pltpu.VMEM((6 * LANES, n_dev * SLOT_ROWS), BF16),
             pltpu.VMEM((640 + n_dev * SLOT_ROWS, 384), BF16),
             pltpu.VMEM((640, n_dev * SLOT_ROWS), BF16),
@@ -847,7 +850,7 @@
         out_specs=(vmem,) * 7,
         compiler_params=pltpu.CompilerParams(vmem_limit_bytes=56 * 1024 * 1024),
     )(*held)
-    return outs[0], outs[1], outs[2], outs[3], outs[4], outs[5].T, outs[6]
+    return outs[0].reshape(whole), outs[1].reshape(whole), outs[2], outs[3], outs[4], outs[5].T, outs[6]
 
 
 def solution(mesh):

time: 45.8 us -> 45.8 us (level)
  no operation moved by 1% of the time
where the time goes in v5:
time: 45.8 us; the launch traced here: 45.7 us
  Pallas kernels  45.1 us (98%)
  between operations  0.65 us (1%)
    pallas_call x1, Pallas kernels, body(): pl.pallas_call(functools.partial(kernel, n_grp, n_dev), out_shape=(packed...  42.5 us
    pallas_call x1, Pallas kernels, body(): pl.pallas_call(finish, out_shape=(packed, packed, jax.ShapeDtypeStruct((7...  2.54 us

profile of v5, /device:TPU:1, one launch (start us, length us, event | category | flops | bytes accessed | tf_op | source)
XLA Modules:
  0.0 45.7 jit_solution(4777281900016487016)
XLA Ops:
  0.6 42.5 %shard_map.180 = (bf16[512,512]{1,0:T(8,128)(2,1)}, bf16[512,512]{1,0:T(8,128)(2,1)}, bf16[1024,128]{1,0:T(8,128)(2,1)}, bf16[256,128]{1,0:T(8,128)(2,1)}, f32[64,128]{1,0:T(8,128)}) custom-call(bf16[512,512]{1,0:T(8,128)(2,1)} %bitcast.8, bf16[512,512]{1,0:T(8,128)(2,1)} %bitcast.9, s32[8]{0:T(128)} %steps_far.1, s32[8,6]{1,0:T(8,128)} %links_far.1, ...), custom_call_target="tpu_custom_call" | custom-call | tf_op jit(solution)/shard_map/pallas_call | solution.py:786
  43.2 2.5 %shard_map.181 = (bf16[512,512]{1,0:T(8,128)(2,1)}, bf16[512,512]{1,0:T(8,128)(2,1)}, f32[7,64,64]{2,1,0:T(8,128)}, f32[64,128]{1,0:T(8,128)}, f32[7,128,128]{2,...) custom-call(bf16[512,512]{1,0:T(8,128)(2,1)} %get-tuple-element.19.mixed_in, ...), custom_call_target="tpu_custom_call" | custom-call | tf_op jit(solution)/shard_map/pallas_call | solution.py:838
